TPU v7x, 512 devices: a whole 4x4x16 slice. The times are simulated.
512 devices in a mesh: ctx: 32 (over z_lo, y), tp: 16 (over z_hi, x, core).
Axes of the slice: x: 4, y: 4, z: 16 (z_hi: 2, z_lo: 8; z = z_hi * 8 + z_lo), core: 2. Of those that a mesh axis runs over, the one named last changes fastest.
Arguments:
- branch_inputs: bfloat16 [3, 6144, 8192], P(None, 'ctx', 'tp'), may hold values from -6 to 6
- feat_taps: bfloat16 [3, 3, 8192], P(None, None, 'tp'), may hold values from -3.5 to 3.5
- long_filter: float32 [128, 8192], P(None, 'tp'), may hold values from -0.5 to 0.5
- out_weight: bfloat16 [8192, 8192], P('tp', 'ctx'), may hold values from -0.0625 to 0.0625
- cotangent: bfloat16 [6144, 8192], P(('ctx', 'tp')), may hold values from -6 to 6
Outputs:
- mixed_out: bfloat16 [6144, 8192], P(('ctx', 'tp'))
- grad_inputs: bfloat16 [3, 6144, 8192], P(None, 'ctx', 'tp')
- grad_filter: float32 [128, 8192], P(None, 'tp')
- grad_taps: float32 [3, 3, 8192], P(None, None, 'tp')
All inputs are finite; a program needn't handle non-finite values.
Results may differ from a plain program's by a relative error of at most 0.03.
Values may be sent and summed in bfloat16 or wider, within the bound.
A program may use at most 64 MiB of HBM per device.

v0:
```python
import jax
import jax.numpy as jnp
from jax import lax
from jax.sharding import PartitionSpec as P


def from_behind(value, axis, steps):
    count = lax.axis_size(axis)
    first, last = (max(0, -steps), min(count, count - steps))
    return lax.ppermute(value, axis, [(source, source + steps) for source in range(first, last)])


def depthwise(signal, kernel):
    result = lax.conv_general_dilated(
        signal[None],
        kernel[:, None, :],
        (1,),
        "VALID",
        dimension_numbers=("NWC", "WIO", "NWC"),
        feature_group_count=signal.shape[1],
        precision=lax.Precision.HIGHEST,
        preferred_element_type=jnp.float32,
    )
    return result[0]


def featurize(raw_rows, kernel_flip):
    return jax.vmap(depthwise)(raw_rows, kernel_flip).astype(jnp.bfloat16)


def body(branch_inputs, feat_taps, long_filter, out_weight, cotangent):
    tok_count = branch_inputs.shape[1]
    chan_count = branch_inputs.shape[2]
    tap_count = feat_taps.shape[1]
    filter_len = long_filter.shape[0]
    short_pad = tap_count - 1
    long_pad = filter_len - 1
    reach_len = long_pad + short_pad
    taps_flip = feat_taps[:, ::-1, :]
    filter_flip = long_filter[::-1]
    tail_rows = jnp.concatenate(
        [
            branch_inputs[0, tok_count - short_pad :],
            branch_inputs[1, tok_count - reach_len :],
            branch_inputs[2, tok_count - reach_len :],
        ],
        axis=0,
    )
    arrived = from_behind(tail_rows, "ctx", 1)
    query_head = arrived[:short_pad]
    key_head = arrived[short_pad : short_pad + reach_len]
    value_head = arrived[short_pad + reach_len :]
    query_feat = featurize(
        jnp.concatenate([query_head, branch_inputs[0]], axis=0)[None], taps_flip[:1]
    )[0]
    key_value = jnp.stack(
        [
            jnp.concatenate([key_head, branch_inputs[1]], axis=0),
            jnp.concatenate([value_head, branch_inputs[2]], axis=0),
        ]
    )
    pair_feat = featurize(key_value, taps_flip[1:])
    pair_full = (pair_feat[0].astype(jnp.float32) * pair_feat[1].astype(jnp.float32)).astype(
        jnp.bfloat16
    )
    key_feat = pair_feat[0, long_pad:]
    value_feat = pair_feat[1, long_pad:]
    raw_heads = jnp.stack([query_head, key_head[long_pad:], value_head[long_pad:]])
    pair_wide = pair_full.astype(jnp.float32)
    long_sum = depthwise(pair_wide, filter_flip)
    query_wide = query_feat.astype(jnp.float32)
    gated_out = (query_wide * long_sum).astype(jnp.bfloat16)
    whole_cotangent = lax.all_gather(cotangent, "tp", axis=0, tiled=True)
    width_total = whole_cotangent.shape[1]
    weight_piece = lax.all_gather(out_weight, "ctx", axis=1, tiled=True)
    partial_out = jnp.zeros((tok_count, width_total), jnp.bfloat16)
    product = jnp.dot(gated_out, weight_piece, preferred_element_type=jnp.float32).astype(
        jnp.bfloat16
    )
    partial_out = lax.dynamic_update_slice_in_dim(partial_out, product, jnp.int32(0), 1)
    grad_sum = lax.dot_general(
        whole_cotangent, weight_piece, (((1,), (1,)), ((), ())), preferred_element_type=jnp.float32
    )
    partial_out, grad_mixed = (partial_out, grad_sum)
    mixed_out = (
        lax.psum_scatter(partial_out, "tp", scatter_dimension=0, tiled=True)
        .astype(jnp.float32)
        .astype(jnp.bfloat16)
    )
    grad_long = grad_mixed * query_wide
    grad_query = grad_mixed * long_sum
    key_wide = key_feat.astype(jnp.float32)
    value_wide = value_feat.astype(jnp.float32)
    taps_wide = feat_taps.astype(jnp.float32)
    pair_lead = depthwise(grad_long[:reach_len], long_filter)
    head_rows = jnp.concatenate(
        [
            grad_long[:long_pad],
            grad_query[:short_pad],
            pair_lead * value_wide[:short_pad],
            pair_lead * key_wide[:short_pad],
        ],
        axis=0,
    )
    arrived_back = from_behind(head_rows.astype(jnp.bfloat16), "ctx", -1).astype(head_rows.dtype)
    grad_pair = depthwise(
        jnp.concatenate([grad_long, arrived_back[:long_pad]], axis=0), long_filter
    )
    grad_feat = jnp.stack([grad_query, grad_pair * value_wide, grad_pair * key_wide])
    feat_full = jnp.concatenate(
        [grad_feat, arrived_back[long_pad:].reshape(3, short_pad, chan_count)], axis=1
    )
    grad_in = jax.vmap(depthwise)(feat_full, taps_wide)
    filter_part = depthwise(pair_wide, grad_long)[::-1]
    raw_full = jnp.concatenate([raw_heads, branch_inputs], axis=1).astype(jnp.float32)
    taps_part = jax.vmap(depthwise)(raw_full, grad_feat)[:, ::-1, :]
    grad_filter, grad_taps = (
        lax.psum(filter_part.astype(jnp.bfloat16), "ctx").astype(jnp.float32),
        lax.psum(taps_part.astype(jnp.bfloat16), "ctx").astype(jnp.float32),
    )
    return (mixed_out, grad_in.astype(jnp.bfloat16), grad_filter, grad_taps)


def solution(mesh):
    placed = (
        P(None, "ctx", "tp"),
        P(None, None, "tp"),
        P(None, "tp"),
        P("tp", "ctx"),
        P(("ctx", "tp"), None),
    )
    return jax.shard_map(
        body,
        mesh=mesh,
        in_specs=placed,
        out_specs=(
            P(("ctx", "tp"), None),
            P(None, "ctx", "tp"),
            P(None, "tp"),
            P(None, None, "tp"),
        ),
        check_vma=False,
    )
```

profile of v0, /device:TPU:6, one launch (start us, length us, event | category | flops | bytes accessed | tf_op | source)
XLA Modules:
  0.0 1084.8 jit_solution(6909744119005020159)
XLA Ops:
  7.3 0.7 all-gather.6.cloned.1.call-update
  8.0 0.7 all-gather.4.cloned.1.call-update
  8.7 0.7 slice_bitcast_fusion.10
  9.4 1.0 slice_bitcast_fusion.7
  10.6 3.5 collective-permute-start
  14.1 0.1 slice.100
  14.2 0.1 slice.106
  14.4 0.1 rev.10
  14.5 1.3 dynamic-slice.4
  16.5 3.2 collective-permute-done
  20.3 0.8 reshape.92
  21.3 0.5 copy.61
  21.9 0.4 reshape.73
  22.3 0.2 reshape.95
  22.5 0.4 copy.63
  23.0 0.4 fusion.3
  23.4 0.4 copy.65
  23.8 0.2 reshape.99
  24.0 0.4 convert_element_type.91
  24.5 0.1 maximum_bitcast_fusion.4
  24.6 0.4 copy.84
  25.1 1.4 reshape.119
  26.6 0.7 copy-done.5
  27.3 4.8 fusion.21
  32.1 101.6 %all-gather.6.cloned.1.call-done = bf16[16,12,8192]{2,1,0:T(8,128)(2,1)} async-done(((bf16[1,12,8192]{2,1,0:T(8,128)(2,1)}), bf16[16,12,8192]{2,1,0:T(8,128)(2,1)}) %all-gather.6.cloned.1.call-update) | async-done | bytes 3145744 | tf_op jit(solution)/shard_map/all_gather | solution.py:73
  133.7 3.2 reshape.118
  136.9 205.3 %all-gather.4.cloned.1.call-done = bf16[512,8192]{1,0:T(8,128)(2,1)} async-done(((bf16[512,256]{1,0:T(8,128)(2,1)}), bf16[512,8192]{1,0:T(8,128)(2,1)}) %all-gather.4.cloned.1.call-update) | async-done | bytes 8388624 | tf_op jit(solution)/shard_map/all_gather | solution.py:75
  342.3 7.3 bitcast_multiply_fusion
  349.6 4.1 fusion.19
  353.8 1.3 rev.11
  355.1 0.7 slice.182
  355.9 0.7 fusion.28
  356.5 0.7 fusion.44
  357.3 0.7 pad_maximum_fusion.1
  357.9 1.5 collective-permute-start.1
  359.4 5.4 convolution_convert_fusion
  364.9 86.7 %fusion = bf16[16,8192]{1,0:T(8,128)(2,1)} fusion(bf16[192,8192]{1,0:T(8,128)(2,1)S(1)} %convolution_convert_fusion), kind=kCustom, calls=%all-reduce-scatter | all-reduce-scatter fusion | flops 2097153 | bytes 3409920
  451.5 1.8 slice.150
  453.3 17.4 %collective-permute-start.4 = (bf16[16,8192]{1,0:T(8,128)(2,1)}, bf16[16,8192]{1,0:T(8,128)(2,1)S(1)}, u32[]{:S(2)}, u32[]{:S(2)}) collective-permute-start(bf16[16,8192]{1,0:T(8,128)(2,1)} %fusion), channel_id=1, source_target_pairs={{0,3},{1,4},{2,5},{3,6},{4,7},{5,8},{6,9},{7,10},{8,11},{9,12},{10... | collective-permute-start | bytes 786440
  470.7 17.2 %collective-permute-start.3 = (bf16[16,8192]{1,0:T(8,128)(2,1)}, bf16[16,8192]{1,0:T(8,128)(2,1)S(1)}, u32[]{:S(2)}, u32[]{:S(2)}) collective-permute-start(bf16[16,8192]{1,0:T(8,128)(2,1)} %fusion), channel_id=1, source_target_pairs={{0,2},{1,3},{2,4},{3,5},{4,6},{5,7},{6,8},{7,9},{8,10},{9,11},{10,... | collective-permute-start | bytes 786440
  487.9 1.9 collective-permute-start.2
  489.8 1.9 collective-permute-start.5
  491.7 324.9 %all-reduce.4.cloned.1.call-done = bf16[128,512]{1,0:T(8,128)(2,1)} async-done(((bf16[128,512]{1,0:T(8,128)(2,1)}), bf16[128,512]{1,0:T(8,128)(2,1)}) %all-reduce.4.cloned.1.call-update) | async-done | bytes 131088 | tf_op jit(solution)/shard_map/psum | solution.py:118
  816.6 1.6 convert_element_type.108
  818.2 0.7 slice.145
  819.0 0.9 slice.142
  820.0 4.1 fusion.17
  824.3 0.9 copy-done.3
  825.2 0.8 copy.85
  826.0 2.5 reshape.120
  828.6 4.3 convolution_reduce_fusion
  833.0 0.8 copy.77
  833.8 0.9 reshape.78
  834.8 1.5 reshape.102
  836.4 0.6 copy-done.10
  837.0 0.3 fusion.1
  837.3 0.2 copy.81
  837.5 0.2 reshape.106
  837.8 0.4 convert_element_type.104
  838.2 0.9 copy.88
  839.2 231.9 %psum.15 = bf16[3,3,512]{2,0,1:T(4,128)(2,1)S(1)} all-reduce(bf16[3,3,512]{2,0,1:T(4,128)(2,1)S(1)} %rev.14), channel_id=1, replica_groups=mesh['ctx'=32,'tp'=16] {'ctx'}, use_global_device_ids=true, to_apply=%region_2.0 | all-reduce | flops 4608 | bytes 18432 | tf_op jit(solution)/shard_map/psum | solution.py:119
  1071.1 0.6 copy.89
  1071.7 5.8 concatenate.36
  1077.5 0.8 constant_dynamic-slice_fusion
  (68 shorter events, 2.0 us)
Async XLA Ops:
  7.2 9.3 copy-start.2
  7.2 6.9 slice-start
  7.2 7.0 slice-start.1
  7.2 7.2 copy-start.7
  7.2 126.5 %all-gather.6.cloned.1.call-start = ((), (), s32[]{:S(2)}) async-start(), calls=%async_computation.2 | async-start | bytes 4456448 | tf_op jit(solution)/shard_map/all_gather | solution.py:73
  7.9 334.3 %all-gather.4.cloned.1.call-start = ((), (), s32[]{:S(2)}) async-start(), calls=%async_computation | async-start | bytes 8650752 | tf_op jit(solution)/shard_map/all_gather | solution.py:75
  8.7 807.9 %all-reduce.4.cloned.1.call-start = ((), (), s32[]{:S(2)}) async-start(), calls=%async_computation.1 | async-start | bytes 262144 | tf_op jit(solution)/shard_map/psum | solution.py:118
  10.6 9.2 collective-permute-start
  16.5 3.6 copy-start.12
  22.3 0.7 copy-start.11
  24.5 2.0 copy-start
  26.6 0.8 copy-start.5
  342.3 7.3 copy-start.6
  349.6 6.3 copy-start.8
  357.9 460.3 %collective-permute-start.1 = (bf16[133,512]{1,0:T(8,128)(2,1)}, bf16[133,512]{1,0:T(8,128)(2,1)}, u32[]{:S(2)}, u32[]{:S(2)}) collective-permute-start(bf16[133,512]{1,0:T(8,128)(2,1)} %pad_maximum_fusion.1), channel_id=1, source_target_pairs={{16,0},{32,16},{48,32},{64,48},{80,64},{96,80},{112,96},{128,112},... | collective-permute-start | bytes 408584 | tf_op jit(solution)/shard_map/ppermute | solution.py:10
  451.5 368.4 %copy-start.9 = (f32[128,512]{1,0:T(8,128)S(1)}, f32[128,512]{1,0:T(8,128)}, u32[]{:S(2)}) copy-start(f32[128,512]{1,0:T(8,128)} %param.7) | copy-start | bytes 786436
  453.3 618.4 %collective-permute-start.4 = (bf16[16,8192]{1,0:T(8,128)(2,1)}, bf16[16,8192]{1,0:T(8,128)(2,1)S(1)}, u32[]{:S(2)}, u32[]{:S(2)}) collective-permute-start(bf16[16,8192]{1,0:T(8,128)(2,1)} %fusion), channel_id=1, source_target_pairs={{0,3},{1,4},{2,5},{3,6},{4,7},{5,8},{6,9},{7,10},{8,11},{9,12},{10... | collective-permute-start | bytes 786440
  470.7 601.0 %collective-permute-start.3 = (bf16[16,8192]{1,0:T(8,128)(2,1)}, bf16[16,8192]{1,0:T(8,128)(2,1)S(1)}, u32[]{:S(2)}, u32[]{:S(2)}) collective-permute-start(bf16[16,8192]{1,0:T(8,128)(2,1)} %fusion), channel_id=1, source_target_pairs={{0,2},{1,3},{2,4},{3,5},{4,6},{5,7},{6,8},{7,9},{8,10},{9,11},{10,... | collective-permute-start | bytes 786440
  487.9 583.8 %collective-permute-start.2 = (bf16[16,8192]{1,0:T(8,128)(2,1)}, bf16[16,8192]{1,0:T(8,128)(2,1)}, u32[]{:S(2)}, u32[]{:S(2)}) collective-permute-start(bf16[16,8192]{1,0:T(8,128)(2,1)} %fusion), channel_id=1, source_target_pairs={{0,1},{1,2},{2,3},{3,4},{4,5},{5,6},{6,7},{7,8},{8,9},{9,10},{10,1... | collective-permute-start | bytes 786440
  489.8 581.9 %collective-permute-start.5 = (bf16[12,8192]{1,0:T(8,128)(2,1)}, bf16[12,8192]{1,0:T(8,128)(2,1)}, u32[]{:S(2)}, u32[]{:S(2)}) collective-permute-start(bf16[12,8192]{1,0:T(8,128)(2,1)} %slice.150), channel_id=1, source_target_pairs={{0,4},{1,5},{2,6},{3,7},{4,8},{5,9},{6,10},{7,11},{8,12},{9,13},{1... | collective-permute-start | bytes 589832
  820.0 4.2 copy-start.1
  824.1 1.0 copy-start.3
  836.2 0.7 copy-start.10
  837.7 234.0 %copy-start.4 = (bf16[16,8192]{1,0:T(8,128)(2,1)S(1)}, bf16[16,8192]{1,0:T(8,128)(2,1)}, u32[]{:S(2)}) copy-start(bf16[16,8192]{1,0:T(8,128)(2,1)} %fusion) | copy-start | bytes 786436
Sparse Core Ops, SparseCore 0:
  11.4 122.2 all-gather.5
  135.7 206.5 all-gather.3
  355.3 461.2 all-reduce.3
where the time goes:
time: 1090 us; the launch traced here: 1080 us
  waiting for transfers between devices  636 us (58%)
  blocking collectives  319 us (29%)
  starting transfers between devices  43.5 us (4%)
  local copies, waits for them, and re-layouts  35.8 us (3%)
  matrix products  31.5 us (3%)
  between operations  15 us (1%)
    psum x1, waiting for transfers between devices, body(): lax.psum(filter_part.astype(jnp.bfloat16), 'ctx').astype(jnp.float32)  325 us
    psum x1, blocking collectives, body(): lax.psum(taps_part.astype(jnp.bfloat16), 'ctx').astype(jnp.float32)  232 us
    all_gather x1, waiting for transfers between devices, body(): weight_piece = lax.all_gather(out_weight, 'ctx', axis=1, tiled=True)  205 us
    all_gather x1, waiting for transfers between devices, body(): whole_cotangent = lax.all_gather(cotangent, 'tp', axis=0, tiled=True)  102 us
    unnamed x1, blocking collectives  86.7 us
    unnamed x4, starting transfers between devices  38.4 us
  transfers between devices with their start and end apart: 9, of which 4 were waited for; matrix products, arithmetic and copies ran while one was open for 13% of the time, Pallas kernels for 0%

commit v1 on v0

--- a/solution.py
+++ b/solution.py
@@ -1,13 +1,417 @@
+import functools
+
 import jax
 import jax.numpy as jnp
 from jax import lax
+from jax.experimental import pallas as pl
+from jax.experimental.pallas import tpu as pltpu
 from jax.sharding import PartitionSpec as P
+
+MESH = pl.DeviceIdType.MESH
+NZ, NY, NX = 8, 4, 4
+
+
+def coords():
+    ctx = lax.axis_index("ctx")
+    tp = lax.axis_index("tp")
+    return ctx, tp, ctx // NY, ctx % NY, tp // (2 * NX), (tp // 2) % NX, tp % 2
+
+
+def device(zl, y, zh, x, c):
+    return {"ctx": zl * NY + y, "tp": zh * (2 * NX) + x * 2 + c}
+
+
+def remote(src, dst, send, recv, target):
+    return pltpu.make_async_remote_copy(
+        src_ref=src, dst_ref=dst, send_sem=send, recv_sem=recv, device_id=target, device_id_type=MESH
+    )
+
+
+def greet(targets):
+    barrier = pltpu.get_barrier_semaphore()
+    count = 0
+    for target, there in targets:
+        if there is True:
+            pl.semaphore_signal(barrier, inc=1, device_id=target, device_id_type=MESH)
+            count = count + 1
+        else:
+            @pl.when(there)
+            def _():
+                pl.semaphore_signal(barrier, inc=1, device_id=target, device_id_type=MESH)
+
+            count = count + there.astype(jnp.int32)
+    pl.semaphore_wait(barrier, count)
+
+
+def gather_kernel(
+    w_ref, cot_ref, tail_ref, wg, cg, halo,
+    own_sem, sib_s, sib_r, z_s, z_r, y_s, y_r, zp_s, zp_r, x_s, x_r, halo_s, halo_r,
+):
+    ctx, tp, zl, y, zh, x, c = coords()
+    right = (zl + 1, y, zh, x, c)
+    left = (zl - 1, y, zh, x, c)
+    yp = device(zl, (y + 1) % NY, zh, x, c)
+    ym = device(zl, (y + 3) % NY, zh, x, c)
+    zpart = device(zl, y, 1 - zh, x, c)
+    sib = device(zl, y, zh, x, 1 - c)
+    xs = [device(zl, y, zh, (x + k) % NX, c) for k in (1, 2, 3)]
+    nxt = {"ctx": jnp.minimum(ctx + 1, NZ * NY - 1), "tp": tp}
+    prv = {"ctx": jnp.maximum(ctx - 1, 0), "tp": tp}
+    dright = device(jnp.minimum(zl + 1, NZ - 1), y, zh, x, c)
+    dleft = device(jnp.maximum(zl - 1, 0), y, zh, x, c)
+    greet(
+        [(sib, True), (yp, True), (ym, True), (zpart, True)]
+        + [(d, True) for d in xs]
+        + [(dright, zl < NZ - 1), (dleft, zl > 0), (nxt, ctx < NZ * NY - 1), (prv, ctx > 0)]
+    )
+    rows = w_ref.shape[0]
+
+    def unit(zs, yy, h):
+        return wg.at[zs * NY + yy, pl.ds(pl.multiple_of(h * rows, rows), rows)]
+
+    keep = w_ref.at[:, pl.ds(pl.multiple_of(c * 128, 128), 128)]
+    give = w_ref.at[:, pl.ds(pl.multiple_of((1 - c) * 128, 128), 128)]
+    w_sib = remote(give, unit(zl, y, c), sib_s.at[0], sib_r.at[0], sib)
+    w_sib.start()
+    w_own = pltpu.make_async_copy(keep, unit(zl, y, c), own_sem.at[0])
+    w_own.start()
+    halo_copy = remote(tail_ref, halo, halo_s, halo_r, nxt)
+
+    @pl.when(ctx < NZ * NY - 1)
+    def _():
+        halo_copy.start()
+
+    c_sib = remote(cot_ref.at[1 - c], cg.at[tp], sib_s.at[1], sib_r.at[1], sib)
+    c_sib.start()
+    c_own = pltpu.make_async_copy(cot_ref.at[c], cg.at[tp], own_sem.at[1])
+    c_own.start()
+
+    def z_right(zs, h):
+        return remote(unit(zs, y, h), unit(zs, y, h), z_s.at[0, zs, h], z_r.at[zs, h], dright)
+
+    def z_left(zs, h):
+        return remote(unit(zs, y, h), unit(zs, y, h), z_s.at[1, zs, h], z_r.at[zs, h], dleft)
+
+    def y_plus(zs, yy, h, kind):
+        return remote(unit(zs, yy, h), unit(zs, yy, h), y_s.at[kind, zs, h], y_r.at[kind, zs, h], yp)
+
+    def y_minus(zs, yy, h, kind):
+        return remote(unit(zs, yy, h), unit(zs, yy, h), y_s.at[kind, zs, h], y_r.at[kind, zs, h], ym)
+
+    def spread(zs, h):
+        y_plus(zs, y, h, 0).start()
+        y_minus(zs, y, h, 1).start()
+
+    def relay(zs, h):
+        y_plus(zs, (y + 3) % NY, h, 0).wait_recv()
+        y_minus(zs, (y + 1) % NY, h, 1).wait_recv()
+
+        @pl.when(h == 0)
+        def _():
+            y_plus(zs, (y + 3) % NY, h, 2).start()
+
+        @pl.when(h == 1)
+        def _():
+            y_minus(zs, (y + 1) % NY, h, 2).start()
+
+    def cot_z(k):
+        piece = zh * (2 * NX) + x * 2 + k
+        return remote(cg.at[piece], cg.at[piece], zp_s.at[k], zp_r.at[k], zpart)
+
+    def cot_x(half, k, n):
+        piece = half * (2 * NX) + x * 2 + k
+        return remote(cg.at[piece], cg.at[piece], x_s.at[half, k, n], x_r.at[half, k, n], xs[n])
+
+    def cot_spread(half, k):
+        for n in range(3):
+            cot_x(half, k, n).start()
+
+    c_own.wait()
+    cot_z(c).start()
+    cot_spread(zh, c)
+    w_own.wait()
+    order = (c, 1 - c)
+    for step in range(NZ):
+        for h in order:
+            if step == 0:
+                if h is not c:
+                    w_sib.wait()
+
+                @pl.when(zl < NZ - 1)
+                def _(h=h):
+                    z_right(zl, h).start()
+
+                @pl.when(zl > 0)
+                def _(h=h):
+                    z_left(zl, h).start()
+
+                spread(zl, h)
+            else:
+                @pl.when(zl - step >= 0)
+                def _(h=h, step=step):
+                    z_right(zl - step, h).wait_recv()
+
+                    @pl.when(zl < NZ - 1)
+                    def _():
+                        z_right(zl - step, h).start()
+
+                    spread(zl - step, h)
+
+                @pl.when(zl + step < NZ)
+                def _(h=h, step=step):
+                    z_left(zl + step, h).wait_recv()
+
+                    @pl.when(zl > 0)
+                    def _():
+                        z_left(zl + step, h).start()
+
+                    spread(zl + step, h)
+        if step == 0:
+            c_sib.wait()
+            cot_z(1 - c).start()
+            cot_spread(zh, 1 - c)
+        if step == 5:
+            for k in order:
+                cot_z(k).wait_recv()
+                cot_spread(1 - zh, k)
+        if step >= 1:
+            for h in order:
+                if step == 1:
+                    relay(zl, h)
+                else:
+                    @pl.when(zl - step + 1 >= 0)
+                    def _(h=h, step=step):
+                        relay(zl - step + 1, h)
+
+                    @pl.when(zl + step - 1 < NZ)
+                    def _(h=h, step=step):
+                        relay(zl + step - 1, h)
+    for h in order:
+        @pl.when(zl == NZ - 1)
+        def _(h=h):
+            relay(0, h)
+
+        @pl.when(zl == 0)
+        def _(h=h):
+            relay(NZ - 1, h)
+
+    @pl.loop(0, NZ)
+    def _(zs):
+        for h in (0, 1):
+            y_plus(zs, (y + 2) % NY, h, 2).wait_recv()
+            y_plus(zs, y, h, 0).wait_send()
+            y_minus(zs, y, h, 1).wait_send()
+            y_plus(zs, y, h, 2).wait_send()
+
+            @pl.when((zs <= zl) & (zl < NZ - 1))
+            def _():
+                z_right(zs, h).wait_send()
+
+            @pl.when((zs >= zl) & (zl > 0))
+            def _():
+                z_left(zs, h).wait_send()
+
+    for k in (0, 1):
+        cot_z(k).wait_send()
+        for half in (0, 1):
+            for n in range(3):
+                cot_x(half, k, n).wait()
+
+    @pl.when(ctx < NZ * NY - 1)
+    def _():
+        halo_copy.wait_send()
+
+    @pl.when(ctx > 0)
+    def _():
+        halo_copy.wait_recv()
+
+
+def gather(weight, cot, tail):
+    rows = weight.shape[0]
+    dma = pltpu.SemaphoreType.DMA
+    any_space = pl.BlockSpec(memory_space=pl.ANY)
+    vmem = pl.BlockSpec(memory_space=pltpu.VMEM)
+    return pl.pallas_call(
+        gather_kernel,
+        out_shape=(
+            jax.ShapeDtypeStruct((NZ * NY, 2 * rows, 128), jnp.bfloat16),
+            jax.ShapeDtypeStruct((4 * NX,) + cot.shape[1:], jnp.bfloat16),
+            jax.ShapeDtypeStruct(tail.shape, jnp.bfloat16),
+        ),
+        in_specs=[vmem, vmem, vmem],
+        out_specs=(any_space, any_space, any_space),
+        scratch_shapes=[
+            dma((2,)), dma((2,)), dma((2,)),
+            dma((2, NZ, 2)), dma((NZ, 2)), dma((3, NZ, 2)), dma((3, NZ, 2)),
+            dma((2,)), dma((2,)), dma((2, 2, 3)), dma((2, 2, 3)),
+            dma, dma,
+        ],
+        compiler_params=pltpu.CompilerParams(collective_id=0, has_side_effects=True),
+        name="gather_weight_cotangent",
+    )(weight, cot, tail)
+
+
+def reduce_kernel(p_ref, o_ref, xbuf, zsend, zbuf, own, x_s, x_r, zp_s, zp_r, sib_s, sib_r):
+    ctx, tp, zl, y, zh, x, c = coords()
+    zpart = device(zl, y, 1 - zh, x, c)
+    sib = device(zl, y, zh, x, 1 - c)
+    xs = [device(zl, y, zh, (x + k) % NX, c) for k in (1, 2, 3)]
+    greet([(sib, True), (zpart, True)] + [(d, True) for d in xs])
+    half = p_ref.shape[2] // 2
+
+    def to_x(zz, n, k):
+        return remote(
+            p_ref.at[zz, (x + n + 1) % NX, pl.ds(k * half, half)], xbuf.at[zz, n, pl.ds(k * half, half)],
+            x_s.at[zz, n, k], x_r.at[zz, n, k], xs[n],
+        )
+
+    for zz in (1 - zh, zh):
+        for k in (0, 1):
+            for n in range(3):
+                to_x(zz, n, k).start()
+
+    def total(zz, k):
+        for n in range(3):
+            to_x(zz, n, k).wait_recv()
+        rows = pl.ds(k * half, half)
+        value = p_ref[zz, x, rows].astype(jnp.float32)
+        for n in range(3):
+            value = value + xbuf[zz, n, rows].astype(jnp.float32)
+        return value
+
+    def to_z(k):
+        return remote(zsend.at[k], zbuf.at[k], zp_s.at[k], zp_r.at[k], zpart)
+
+    for k in (0, 1):
+        zsend[k] = total(1 - zh, k).astype(jnp.bfloat16)
+        to_z(k).start()
+    for k in (0, 1):
+        own[k] = total(zh, k)
+    for k in (0, 1):
+        to_z(k).wait_recv()
+        own[k] = own[k] + zbuf[k].astype(jnp.float32)
+    to_z(0).wait_send()
+    to_z(1).wait_send()
+    zsend[0] = own[1 - c].astype(jnp.bfloat16)
+    o_ref[c] = own[c].astype(jnp.bfloat16)
+    last = remote(zsend.at[0], o_ref.at[c], sib_s, sib_r, sib)
+    last.start()
+    last.wait()
+    for zz in (0, 1):
+        for k in (0, 1):
+            for n in range(3):
+                to_x(zz, n, k).wait_send()
+
+
+def reduce_out(partial):
+    dma = pltpu.SemaphoreType.DMA
+    rows, cols = partial.shape[2:]
+    half = rows // 2
+    vmem = pl.BlockSpec(memory_space=pltpu.VMEM)
+    return pl.pallas_call(
+        reduce_kernel,
+        out_shape=jax.ShapeDtypeStruct((2, half, cols), jnp.bfloat16),
+        in_specs=[vmem],
+        out_specs=vmem,
+        scratch_shapes=[
+            pltpu.VMEM((2, 3, rows, cols), jnp.bfloat16),
+            pltpu.VMEM((2, half, cols), jnp.bfloat16),
+            pltpu.VMEM((2, half, cols), jnp.bfloat16),
+            pltpu.VMEM((2, half, cols), jnp.float32),
+            dma((2, 3, 2)), dma((2, 3, 2)), dma((2,)), dma((2,)), dma, dma,
+        ],
+        compiler_params=pltpu.CompilerParams(
+            collective_id=1, has_side_effects=True, vmem_limit_bytes=32 * 2**20
+        ),
+        name="reduce_block_out",
+    )(partial)
+
+
+def sum_kernel(f_ref, o_ref, mine, ybuf, zbuf, y_s, y_r, z_s, z_r, t_s, t_r, g_s, g_r, e_s, e_r):
+    ctx, tp, zl, y, zh, x, c = coords()
+    ys = [device(zl, (y + k) % NY, zh, x, c) for k in (1, 2, 3)]
+    zs = [device((zl + k) % NZ, y, zh, x, c) for k in range(1, NZ)]
+    greet([(d, True) for d in ys + zs])
+
+    def to_y(n):
+        return remote(f_ref.at[(y + n + 1) % NY], ybuf.at[n], y_s.at[n], y_r.at[n], ys[n])
+
+    def to_z(n):
+        return remote(mine.at[(zl + n + 1) % NZ], zbuf.at[n, 0], z_s.at[n], z_r.at[n], zs[n])
+
+    def taps_z(n):
+        return remote(mine.at[NZ], zbuf.at[n, 1], t_s.at[n], t_r.at[n], zs[n])
+
+    def back_z(n):
+        return remote(o_ref.at[y, zl], o_ref.at[y, zl], g_s.at[n], g_r.at[n], zs[n])
+
+    def back_y(n):
+        return remote(o_ref.at[y], o_ref.at[y], e_s.at[n], e_r.at[n], ys[n])
+
+    for n in range(3):
+        to_y(n).start()
+    value = f_ref[y].astype(jnp.float32)
+    for n in range(3):
+        to_y(n).wait_recv()
+        value = value + ybuf[n].astype(jnp.float32)
+    mine[...] = value.astype(jnp.bfloat16)
+    for n in range(NZ - 1):
+        to_z(n).start()
+        taps_z(n).start()
+    value = mine[zl].astype(jnp.float32)
+    taps = mine[NZ].astype(jnp.float32)
+    for n in range(NZ - 1):
+        to_z(n).wait_recv()
+        taps_z(n).wait_recv()
+        value = value + zbuf[n, 0].astype(jnp.float32)
+        taps = taps + zbuf[n, 1].astype(jnp.float32)
+    o_ref[y, zl] = value.astype(jnp.bfloat16)
+    o_ref[y, NZ] = taps.astype(jnp.bfloat16)
+    for n in range(NZ - 1):
+        back_z(n).start()
+    for n in range(NZ - 1):
+        back_z(n).wait()
+    for n in range(3):
+        back_y(n).start()
+    for n in range(3):
+        back_y(n).wait()
+    for n in range(3):
+        to_y(n).wait_send()
+    for n in range(NZ - 1):
+        to_z(n).wait_send()
+        taps_z(n).wait_send()
+
+
+def sum_gradients(parts):
+    dma = pltpu.SemaphoreType.DMA
+    vmem = pl.BlockSpec(memory_space=pltpu.VMEM)
+    tile = parts.shape[1:]
+    return pl.pallas_call(
+        sum_kernel,
+        out_shape=jax.ShapeDtypeStruct(parts.shape, jnp.bfloat16),
+        in_specs=[vmem],
+        out_specs=vmem,
+        scratch_shapes=[
+            pltpu.VMEM(tile, jnp.bfloat16),
+            pltpu.VMEM((3,) + tile, jnp.bfloat16),
+            pltpu.VMEM((NZ - 1, 2) + tile[1:], jnp.bfloat16),
+            dma((3,)), dma((3,)), dma((NZ - 1,)), dma((NZ - 1,)), dma((NZ - 1,)), dma((NZ - 1,)),
+            dma((NZ - 1,)), dma((NZ - 1,)), dma((3,)), dma((3,)),
+        ],
+        compiler_params=pltpu.CompilerParams(collective_id=2, has_side_effects=True),
+        name="sum_filter_gradients",
+    )(parts)
 
 
 def from_behind(value, axis, steps):
     count = lax.axis_size(axis)
     first, last = (max(0, -steps), min(count, count - steps))
     return lax.ppermute(value, axis, [(source, source + steps) for source in range(first, last)])
+
+
+def from_sibling(value):
+    count = lax.axis_size("tp")
+    return lax.ppermute(value, "tp", [(k, k ^ 1) for k in range(count)])
 
 
 def depthwise(signal, kernel):
@@ -38,18 +442,26 @@
     reach_len = long_pad + short_pad
     taps_flip = feat_taps[:, ::-1, :]
     filter_flip = long_filter[::-1]
+    core = lax.axis_index("tp") % 2
     tail_rows = jnp.concatenate(
         [
             branch_inputs[0, tok_count - short_pad :],
             branch_inputs[1, tok_count - reach_len :],
             branch_inputs[2, tok_count - reach_len :],
+            jnp.zeros((12, chan_count), jnp.bfloat16),
         ],
         axis=0,
     )
-    arrived = from_behind(tail_rows, "ctx", 1)
+    own_rows = cotangent.shape[0]
+    width = cotangent.shape[1]
+    cot_halves = (
+        cotangent.reshape(own_rows, 4, 8, 2, 128).transpose(3, 1, 0, 2, 4).reshape(2, 4 * own_rows, 1024)
+    )
+    weight_all, cot_all, arrived = gather(out_weight, cot_halves, tail_rows)
+    arrived = jnp.where(lax.axis_index("ctx") > 0, arrived, jnp.zeros_like(arrived))
     query_head = arrived[:short_pad]
     key_head = arrived[short_pad : short_pad + reach_len]
-    value_head = arrived[short_pad + reach_len :]
+    value_head = arrived[short_pad + reach_len : short_pad + 2 * reach_len]
     query_feat = featurize(
         jnp.concatenate([query_head, branch_inputs[0]], axis=0)[None], taps_flip[:1]
     )[0]
@@ -70,23 +482,26 @@
     long_sum = depthwise(pair_wide, filter_flip)
     query_wide = query_feat.astype(jnp.float32)
     gated_out = (query_wide * long_sum).astype(jnp.bfloat16)
-    whole_cotangent = lax.all_gather(cotangent, "tp", axis=0, tiled=True)
-    width_total = whole_cotangent.shape[1]
-    weight_piece = lax.all_gather(out_weight, "ctx", axis=1, tiled=True)
-    partial_out = jnp.zeros((tok_count, width_total), jnp.bfloat16)
-    product = jnp.dot(gated_out, weight_piece, preferred_element_type=jnp.float32).astype(
-        jnp.bfloat16
-    )
-    partial_out = lax.dynamic_update_slice_in_dim(partial_out, product, jnp.int32(0), 1)
-    grad_sum = lax.dot_general(
-        whole_cotangent, weight_piece, (((1,), (1,)), ((), ())), preferred_element_type=jnp.float32
-    )
-    partial_out, grad_mixed = (partial_out, grad_sum)
-    mixed_out = (
-        lax.psum_scatter(partial_out, "tp", scatter_dimension=0, tiled=True)
-        .astype(jnp.float32)
-        .astype(jnp.bfloat16)
-    )
+    other_out = from_sibling(gated_out)
+    both_out = jnp.where(
+        core == 0,
+        jnp.concatenate([gated_out, other_out], axis=1),
+        jnp.concatenate([other_out, gated_out], axis=1),
+    )
+    product = jnp.einsum("tc,bcl->tbl", both_out, weight_all, preferred_element_type=jnp.float32)
+    partial = (
+        product.astype(jnp.bfloat16)
+        .reshape(2, 4, 2, own_rows, 4, 1024)
+        .transpose(0, 1, 2, 4, 3, 5)
+        .reshape(2, 4, 8 * own_rows, 1024)
+    )
+    mixed = reduce_out(partial)
+    mixed_out = mixed.reshape(2, 4, own_rows, 8, 128).transpose(2, 1, 3, 0, 4).reshape(own_rows, width)
+    cot_half = cot_all.reshape(16, 4, own_rows, 8, 128).transpose(0, 2, 1, 3, 4).reshape(tok_count, 32, 128)
+    grad_both = jnp.einsum("tbl,bcl->tc", cot_half, weight_all, preferred_element_type=jnp.float32)
+    grad_own = lax.dynamic_slice_in_dim(grad_both, core * chan_count, chan_count, 1)
+    grad_other = lax.dynamic_slice_in_dim(grad_both, (1 - core) * chan_count, chan_count, 1)
+    grad_mixed = grad_own + from_sibling(grad_other)
     grad_long = grad_mixed * query_wide
     grad_query = grad_mixed * long_sum
     key_wide = key_feat.astype(jnp.float32)
@@ -114,10 +529,13 @@
     filter_part = depthwise(pair_wide, grad_long)[::-1]
     raw_full = jnp.concatenate([raw_heads, branch_inputs], axis=1).astype(jnp.float32)
     taps_part = jax.vmap(depthwise)(raw_full, grad_feat)[:, ::-1, :]
-    grad_filter, grad_taps = (
-        lax.psum(filter_part.astype(jnp.bfloat16), "ctx").astype(jnp.float32),
-        lax.psum(taps_part.astype(jnp.bfloat16), "ctx").astype(jnp.float32),
-    )
+    parts = jnp.concatenate(
+        [filter_part, taps_part.reshape(9, chan_count), jnp.zeros((7, chan_count), jnp.float32)], axis=0
+    ).astype(jnp.bfloat16)
+    sums = sum_gradients(parts.reshape(9, 16, 4, 128).transpose(2, 0, 1, 3))
+    sums = sums.transpose(1, 2, 0, 3).reshape(144, chan_count).astype(jnp.float32)
+    grad_filter = sums[:filter_len]
+    grad_taps = sums[filter_len : filter_len + 9].reshape(3, tap_count, chan_count)
     return (mixed_out, grad_in.astype(jnp.bfloat16), grad_filter, grad_taps)
 
 

time: 1090 us -> 249 us (0.23)
  waiting for transfers between devices: 636 us -> 1.83 us
  blocking collectives: 319 us -> 0 us
  Pallas kernels: 0 us -> 165 us
  starting transfers between devices: 43.5 us -> 5.79 us
  between operations: 15 us -> 1.32 us
    psum x1 -> x0, waiting for transfers between devices: 325 us -> none  [body(): lax.psum(filter_part.astype(jnp.bfloat16), 'ctx').astype(jnp.float32)]
    all_gather x2 -> x0, waiting for transfers between devices: 307 us -> none  [the longest x1 205 us: body(): weight_piece = lax.all_gather(out_weight, 'ctx', axis=1, tiled=True)]
    psum x1 -> x0, blocking collectives: 232 us -> none  [body(): lax.psum(taps_part.astype(jnp.bfloat16), 'ctx').astype(jnp.float32)]
    pallas_call x0 -> x3, Pallas kernels: none -> 165 us  [the longest x1 104 us: gather(): pl.pallas_call(gather_kernel, out_shape=(jax.ShapeDtypeStruct((NZ * NY, 2...]
    unnamed x1 -> x0, blocking collectives: 86.7 us -> none
    unnamed x4 -> x0, starting transfers between devices: 38.4 us -> none
  transfers between devices with their start and end apart: 9 -> 3, of which waited for: 4 -> 1; matrix products, arithmetic and copies ran while one was open for 13% -> 16% of each run, Pallas kernels for 0% -> 13%
where the time goes in v1:
time: 249 us; the launch traced here: 244 us
  Pallas kernels  165 us (66%)
  matrix products  35.9 us (14%)
  local copies, waits for them, and re-layouts  30.2 us (12%)
  starting transfers between devices  5.79 us (2%)
  other arithmetic  4.56 us (2%)
    pallas_call x1, Pallas kernels, gather(): pl.pallas_call(gather_kernel, out_shape=(jax.ShapeDtypeStruct((NZ * NY, 2...  104 us
    pallas_call x1, Pallas kernels, sum_gradients(): pl.pallas_call(sum_kernel, out_shape=jax.ShapeDtypeStruct(parts.shape, jn...  31.3 us
    pallas_call x1, Pallas kernels, reduce_out(): pl.pallas_call(reduce_kernel, out_shape=jax.ShapeDtypeStruct((2, half, co...  29.4 us
    conv_general_dilated x8, matrix products, depthwise(): lax.conv_general_dilated(signal[None], kernel[:, None, :], (1,), 'VALID',...  23.1 us
    reshape x10, local copies, waits for them, and re-layouts, depthwise(): lax.conv_general_dilated(signal[None], kernel[:, None, :], (1,), 'VALID',...  8.03 us
    dot_general x1, matrix products, body(): jnp.einsum('tbl,bcl->tc', cot_half, weight_all, preferred_element_type=jn...  7.23 us
    unnamed x22, local copies, waits for them, and re-layouts  5.94 us
    dot_general x1, matrix products, body(): jnp.einsum('tc,bcl->tbl', both_out, weight_all, preferred_element_type=jn...  5.56 us
  transfers between devices with their start and end apart: 3, of which 1 were waited for; matrix products, arithmetic and copies ran while one was open for 16% of the time, Pallas kernels for 13%

profile of v1, /device:TPU:6, one launch (start us, length us, event | category | flops | bytes accessed | tf_op | source)
XLA Modules:
  0.0 244.5 jit_solution(10764799518763170184)
XLA Ops:
  0.6 1.0 slice_bitcast_fusion.5
  1.7 0.7 slice_bitcast_fusion.8
  2.4 1.1 reshape.109
  3.5 0.8 reshape.110.cot_ref
  4.4 0.8 maximum_maximum_fusion.tail_ref
  5.2 104.1 %gather_weight_cotangent.1 = (bf16[32,1024,128]{2,1,0:T(8,128)(2,1)}, bf16[16,48,1024]{2,1,0:T(8,128)(2,1)}, bf16[272,512]{1,0:T(8,128)(2,1)}) custom-call(bf16[512,256]{1,0:T(8,128)(2,1)} %w_ref.1, bf16[2,48,1024]{2,1,0:T(8,128)(2,1)} %reshape.110.cot_ref, bf16[272,512]{1,0:T(8,128)(2,1)} %maximum_maximum_fusion.tail_ref), custom_call_target="tpu_custom_call" | custom-call | tf_op jit(solution)/shard_map/gather_weight_cotangent/pallas_call | solution.py:234
  109.3 1.8 copy.70
  111.2 0.3 copy.41
  111.5 7.2 %fusion.7 = f32[192,1024]{1,0:T(8,128)} fusion(bf16[32,1024,128]{2,1,0:T(8,128)(2,1)} %get-tuple-element.8, bf16[192,32,128]{2,1,0:T(8,128)(2,1)S(1)} %bitcast.149), kind=kOutput, calls=%fused_computation.11 | convolution fusion | flops 1610612736 | bytes 10747904 | tf_op jit(solution)/shard_map/tbl,bcl->tc/dot_general | solution.py:501
  118.8 1.8 constant_dynamic-slice_fusion
  120.6 2.1 collective-permute-start.1
  123.1 0.5 copy.31
  123.6 0.5 reshape.146
  124.1 0.1 slice-done.1
  124.3 0.1 slice.115
  124.4 4.9 %fusion.11 = bf16[319,1024]{1,0:T(8,128)(2,1)S(1)} fusion(bf16[1,321,1024]{2,0,1:T(2,128)(2,1)S(1)} %reshape.146, bf16[3,1,1024]{2,0,1:T(4,128)(2,1)S(1)} %bitcast.164), kind=kOutput, calls=%fused_computation.17 | convolution fusion | flops 2286592 | bytes 1316864 | tf_op jit(solution)/shard_map/vmap()/conv_general_dilated | solution.py:418
  129.3 0.4 convert_element_type.91
  129.8 0.8 copy-done.4
  130.6 0.1 rev.10
  130.7 4.1 %fusion.18 = f32[1,192,512]{2,0,1:T(1,128)S(1)} fusion(bf16[1,319,512]{2,1,0:T(8,128)(2,1)S(1)} %fusion.31, f32[128,1,512]{2,0,1:T(8,128)S(1)} %bitcast.161), kind=kOutput, calls=%fused_computation.30 | convolution fusion | flops 150994944 | bytes 982016 | tf_op jit(solution)/shard_map/conv_general_dilated | solution.py:418
  134.9 0.1 maximum_bitcast_fusion.4
  135.1 0.5 slice-done.2
  135.7 0.4 copy.58
  136.1 1.4 reshape.147
  137.7 0.6 fusion.10
  138.3 0.5 copy-done.2
  138.8 1.8 bitcast_multiply_fusion
  140.7 2.4 collective-permute-start
  143.1 0.7 fusion.32
  143.8 1.3 collective-permute-start.2
  145.1 4.1 %fusion.16 = bf16[1,128,512]{2,0,1:T(2,128)(2,1)S(1)} fusion(bf16[1,319,512]{2,1,0:T(8,128)(2,1)S(1)} %fusion.31, f32[192,1,512]{2,0,1:T(8,128)S(1)} %bitcast.145), kind=kOutput, calls=%fused_computation.28 | convolution fusion | flops 150994944 | bytes 850944 | tf_op jit(solution)/shard_map/conv_general_dilated | solution.py:418
  149.3 0.2 rev.11
  149.5 1.8 collective-permute-done.2
  151.4 4.1 %fusion.14 = f32[1,192,512]{2,0,1:T(1,128)S(1)} fusion(f32[1,319,512]{2,1,0:T(8,128)S(1)} %maximum_bitcast_fusion.3, f32[128,1,512]{2,0,1:T(8,128)S(1)} %bitcast.159), kind=kOutput, calls=%fused_computation.23 | convolution fusion | flops 150994944 | bytes 1308672 | tf_op jit(solution)/shard_map/conv_general_dilated | solution.py:418
  155.6 0.1 convert_multiply_fusion.1
  155.8 0.8 copy.59
  156.6 2.5 %reshape.148 = f32[192,1,1536]{2,1,0:T(1,128)} reshape(f32[192,1,3,512]{3,2,0,1:T(4,128)S(1)} %copy.59) | data formatting | bytes 2359296 | tf_op jit(solution)/shard_map/vmap()/reshape | solution.py:418
  159.1 4.3 %convolution_reduce_fusion = bf16[3,1536]{1,0:T(4,128)(2,1)S(1)} fusion(bf16[1,194,1536]{2,0,1:T(2,128)(2,1)} %reshape.147, f32[192,1,1536]{2,1,0:T(1,128)} %reshape.148), kind=kOutput, calls=%fused_computation.16 | convolution fusion | flops 10616832 | bytes 1784832 | tf_op jit(solution)/shard_map/vmap()/conv_general_dilated | solution.py:418
  163.6 0.7 copy.126
  164.3 31.3 %sum_filter_gradients.1 = bf16[4,9,16,128]{3,2,1,0:T(8,128)(2,1)} custom-call(bf16[4,9,16,128]{3,2,1,0:T(8,128)(2,1)} %bitcast.155), custom_call_target="tpu_custom_call" | custom-call | tf_op jit(solution)/shard_map/sum_filter_gradients/pallas_call | solution.py:389
  195.6 0.9 convert_bitcast_fusion
  196.5 0.1 copy.65
  196.7 0.1 maximum_bitcast_fusion
  196.8 0.5 copy-done.1
  197.3 0.8 copy.51
  198.1 0.9 reshape.123
  199.1 1.5 reshape.135
  200.7 0.6 copy-done.6
  201.3 0.3 fusion
  201.6 0.2 copy.55
  201.8 0.2 reshape.139
  202.1 0.4 convert_element_type.104
  202.5 0.9 copy.66
  203.5 0.2 copy.64
  203.6 0.7 copy.123
  204.4 0.6 reshape.132
  205.0 5.6 %convolution_convert_fusion = bf16[192,32,128]{2,0,1:T(8,128)(2,1)S(1)} fusion(bf16[32,1024,128]{2,1,0:T(8,128)(2,1)} %get-tuple-element.8, bf16[192,512]{1,0:T(8,128)(2,1)} %collective-permute-done, bf16[192,512]{1,0:T(8,128)(2,1)} %get-tuple-element.18, pred[]{:T(512)S(6)} %eq.5), kind=kOutput, calls=%fused_computation.2 | convolution fusion | flops 1613168640 | bytes 10354689 | tf_op jit(solution)/shard_map/tc,bcl->tbl/dot_general | solution.py:491
  210.6 1.0 copy.37
  211.6 0.7 reshape.115
  212.3 1.2 copy.38
  213.5 0.5 copy.39.p_ref
  214.0 29.4 %reduce_block_out.1 = bf16[2,48,1024]{2,1,0:T(8,128)(2,1)S(1)} custom-call(bf16[2,4,96,1024]{3,2,1,0:T(8,128)(2,1)S(1)} %copy.39.p_ref), custom_call_target="tpu_custom_call" | custom-call | tf_op jit(solution)/shard_map/reduce_block_out/pallas_call | solution.py:311
  243.5 0.2 copy.40
  243.7 0.8 reshape.118
  (57 shorter events, 1.6 us)
Async XLA Ops:
  111.5 11.2 %copy-start = (bf16[3,192,512]{2,1,0:T(8,128)(2,1)S(1)}, bf16[3,192,512]{2,1,0:T(8,128)(2,1)}, u32[]{:S(2)}) copy-start(bf16[3,192,512]{2,1,0:T(8,128)(2,1)} %param.5) | copy-start | bytes 1769476
  118.8 4.0 %copy-start.3 = (bf16[272,512]{1,0:T(8,128)(2,1)S(1)}, bf16[272,512]{1,0:T(8,128)(2,1)}, u32[]{:S(2)}) copy-start(bf16[272,512]{1,0:T(8,128)(2,1)} %get-tuple-element.7) | copy-start | bytes 835588
  120.6 17.7 %collective-permute-start.1 = (f32[192,512]{1,0:T(8,128)}, f32[192,512]{1,0:T(8,128)}, u32[]{:S(2)}, u32[]{:S(2)}) collective-permute-start(f32[192,512]{1,0:T(8,128)} %constant_dynamic-slice_fusion), channel_id=1, source_target_pairs={{0,1},{1,0},{2,3},{3,2},{4,5},{5,4},{6,7},{7,6},{8,9},{9,8},{10,11... | collective-permute-start | bytes 1179656 | tf_op jit(solution)/shard_map/ppermute | solution.py:414
  123.6 0.7 slice-start.1
  129.6 1.0 copy-start.4
  134.9 0.7 slice-start.2
  137.7 1.1 copy-start.2
  140.7 64.3 %collective-permute-start = (bf16[192,512]{1,0:T(8,128)(2,1)}, bf16[192,512]{1,0:T(8,128)(2,1)}, u32[]{:S(2)}, u32[]{:S(2)}) collective-permute-start(bf16[192,512]{1,0:T(8,128)(2,1)} %get-tuple-element.18), channel_id=1, source_target_pairs={{0,1},{1,0},{2,3},{3,2},{4,5},{5,4},{6,7},{7,6},{8,9},{9,8},{10,11... | collective-permute-start | bytes 589832 | tf_op jit(solution)/shard_map/ppermute | solution.py:414
  143.8 7.5 %collective-permute-start.2 = (bf16[133,512]{1,0:T(8,128)(2,1)S(1)}, bf16[133,512]{1,0:T(8,128)(2,1)S(1)}, u32[]{:S(2)}, u32[]{:S(2)}) collective-permute-start(bf16[133,512]{1,0:T(8,128)(2,1)S(1)} %pad_maximum_fusion), channel_id=1, source_target_pairs={{16,0},{32,16},{48,32},{64,48},{80,64},{96,80},{112,96},{128,112},... | collective-permute-start | bytes 408584 | tf_op jit(solution)/shard_map/ppermute | solution.py:409
  149.3 2.1 copy-start.5
  196.5 0.7 copy-start.1
  200.6 0.7 copy-start.6
  200.6 0.7 copy-start.7
  202.1 1.4 slice-start

commit v2 on v0

--- a/solution.py
+++ b/solution.py
@@ -1,13 +1,406 @@
+import functools
+
 import jax
 import jax.numpy as jnp
 from jax import lax
+from jax.experimental import pallas as pl
+from jax.experimental.pallas import tpu as pltpu
 from jax.sharding import PartitionSpec as P
+
+MESH = pl.DeviceIdType.MESH
+NZ, NY, NX = 8, 4, 4
+
+
+def coords():
+    ctx = lax.axis_index("ctx")
+    tp = lax.axis_index("tp")
+    return ctx, tp, ctx // NY, ctx % NY, tp // (2 * NX), (tp // 2) % NX, tp % 2
+
+
+def device(zl, y, zh, x, c):
+    return {"ctx": zl * NY + y, "tp": zh * (2 * NX) + x * 2 + c}
+
+
+def remote(src, dst, send, recv, target):
+    return pltpu.make_async_remote_copy(
+        src_ref=src, dst_ref=dst, send_sem=send, recv_sem=recv, device_id=target, device_id_type=MESH
+    )
+
+
+def greet(targets):
+    barrier = pltpu.get_barrier_semaphore()
+    count = 0
+    for target, there in targets:
+        if there is True:
+            pl.semaphore_signal(barrier, inc=1, device_id=target, device_id_type=MESH)
+            count = count + 1
+        else:
+            @pl.when(there)
+            def _():
+                pl.semaphore_signal(barrier, inc=1, device_id=target, device_id_type=MESH)
+
+            count = count + there.astype(jnp.int32)
+    pl.semaphore_wait(barrier, count)
+
+
+def block_kernel(
+    w_ref, cot_ref, cotz_ref, x_ref, g_ref, s_ref,
+    wg, cg, both, acc, out, arrived, gsend, grecv,
+    own_sem, sib_s, sib_r, z_s, z_r, y_s, y_r, x_s, x_r, o_s, o_r,
+):
+    ctx, tp, zl, y, zh, x, c = coords()
+    yp = device(zl, (y + 1) % NY, zh, x, c)
+    ym = device(zl, (y + 3) % NY, zh, x, c)
+    sib = device(zl, y, zh, x, 1 - c)
+    xs = [device(zl, y, zh, (x + k) % NX, c) for k in (1, 2, 3)]
+    dright = device(jnp.minimum(zl + 1, NZ - 1), y, zh, x, c)
+    dleft = device(jnp.maximum(zl - 1, 0), y, zh, x, c)
+    greet(
+        [(sib, True), (yp, True), (ym, True)]
+        + [(d, True) for d in xs]
+        + [(dright, zl < NZ - 1), (dleft, zl > 0)]
+    )
+    rows = w_ref.shape[0]
+
+    def unit(zs, yy, h):
+        return wg.at[zs * NY + yy, pl.ds(pl.multiple_of(h * rows, rows), rows)]
+
+    keep = w_ref.at[:, pl.ds(pl.multiple_of(c * 128, 128), 128)]
+    give = w_ref.at[:, pl.ds(pl.multiple_of((1 - c) * 128, 128), 128)]
+    w_sib = remote(give, unit(zl, y, c), sib_s.at[0], sib_r.at[0], sib)
+    w_sib.start()
+    w_own = pltpu.make_async_copy(keep, unit(zl, y, c), own_sem.at[0])
+    w_own.start()
+    x_sib = remote(x_ref, both.at[c], sib_s.at[1], sib_r.at[1], sib)
+    x_sib.start()
+    x_own = pltpu.make_async_copy(x_ref, both.at[c], own_sem.at[1])
+    x_own.start()
+    far = (1 - zh) * (2 * NX) + x * 2 + c
+    c_sib = [
+        remote(ref.at[1 - c], cg.at[at], sib_s.at[2 + n], sib_r.at[2 + n], sib)
+        for n, (ref, at) in enumerate(((cot_ref, tp), (cotz_ref, far)))
+    ]
+    c_own = [
+        pltpu.make_async_copy(ref.at[c], cg.at[at], own_sem.at[2 + n])
+        for n, (ref, at) in enumerate(((cot_ref, tp), (cotz_ref, far)))
+    ]
+    for copy in c_sib + c_own:
+        copy.start()
+
+    def z_right(zs, h):
+        return remote(unit(zs, y, h), unit(zs, y, h), z_s.at[0, zs, h], z_r.at[zs, h], dright)
+
+    def z_left(zs, h):
+        return remote(unit(zs, y, h), unit(zs, y, h), z_s.at[1, zs, h], z_r.at[zs, h], dleft)
+
+    def y_plus(zs, yy, h, kind):
+        return remote(unit(zs, yy, h), unit(zs, yy, h), y_s.at[kind, zs, h], y_r.at[kind, zs, h], yp)
+
+    def y_minus(zs, yy, h, kind):
+        return remote(unit(zs, yy, h), unit(zs, yy, h), y_s.at[kind, zs, h], y_r.at[kind, zs, h], ym)
+
+    def spread(zs, h):
+        y_plus(zs, y, h, 0).start()
+        y_minus(zs, y, h, 1).start()
+
+    def relay(zs, h):
+        y_plus(zs, (y + 3) % NY, h, 0).wait_recv()
+        y_minus(zs, (y + 1) % NY, h, 1).wait_recv()
+
+        @pl.when(h == 0)
+        def _():
+            y_plus(zs, (y + 3) % NY, h, 2).start()
+
+        @pl.when(h == 1)
+        def _():
+            y_minus(zs, (y + 1) % NY, h, 2).start()
+
+    def cot_x(half, k, n):
+        piece = half * (2 * NX) + x * 2 + k
+        return remote(cg.at[piece], cg.at[piece], x_s.at[half, k, n], x_r.at[half, k, n], xs[n])
+
+    def out_x(zs, n):
+        return remote(out.at[zs, (x + n + 1) % NX], arrived.at[zs, n], o_s.at[zs, n], o_r.at[zs, n], xs[n])
+
+    order = (c, 1 - c)
+    w_own.wait()
+    for h in order:
+        if h is not c:
+            w_sib.wait()
+
+        @pl.when(zl < NZ - 1)
+        def _(h=h):
+            z_right(zl, h).start()
+
+        @pl.when(zl > 0)
+        def _(h=h):
+            z_left(zl, h).start()
+
+        spread(zl, h)
+    for copy in c_own:
+        copy.wait()
+    for n in range(3):
+        cot_x(zh, c, n).start()
+        cot_x(1 - zh, c, n).start()
+    for copy in c_sib:
+        copy.wait()
+    for n in range(3):
+        cot_x(zh, 1 - c, n).start()
+        cot_x(1 - zh, 1 - c, n).start()
+    x_own.wait()
+    x_sib.wait()
+    acc[...] = jnp.zeros_like(acc)
+
+    def weight(zs, k):
+        return jnp.concatenate([wg[zs * NY + yy, k * rows : (k + 1) * rows] for yy in range(NY)], axis=1)
+
+    def forward(zs):
+        for h in (0, 1):
+            y_plus(zs, (y + 2) % NY, h, 2).wait_recv()
+        value = jnp.dot(both[0], weight(zs, 0), preferred_element_type=jnp.float32)
+        value = value + jnp.dot(both[1], weight(zs, 1), preferred_element_type=jnp.float32)
+        value = value.astype(jnp.bfloat16)
+        for half in (0, 1):
+            for xx in range(NX):
+                at = (half * NX + xx) * 32
+                out[zs, xx, half] = value[at : at + 32]
+        for n in range(3):
+            out_x(zs, n).start()
+
+    def backward(zs):
+        cot = jnp.concatenate([cg[piece, zs] for piece in range(4 * NX)], axis=0)
+        for k in (0, 1):
+            acc[k] += lax.dot_general(
+                cot, weight(zs, k), (((1,), (1,)), ((), ())), preferred_element_type=jnp.float32
+            )
+
+    def collect(zs):
+        value = out[zs, x].astype(jnp.float32)
+        for n in range(3):
+            out_x(zs, n).wait_recv()
+            value = value + arrived[zs, n].astype(jnp.float32)
+        value = value.astype(jnp.bfloat16)
+        for half in (0, 1):
+            for k in (0, 1):
+                s_ref[half, k, zs] = value[half, k * 16 : (k + 1) * 16]
+
+    def both_sides(step, act):
+        @pl.loop(0, 2)
+        def _(side):
+            zs = zl + (2 * side - 1) * step
+
+            @pl.when((step >= 0) & (zs >= 0) & (zs < NZ) & ((step > 0) | (side == 0)))
+            def _():
+                act(zs)
+
+    @pl.loop(1, NZ + 2)
+    def _(step):
+        for h in order:
+            @pl.when((zl - step >= 0) & (step < NZ))
+            def _(h=h):
+                z_right(zl - step, h).wait_recv()
+
+                @pl.when(zl < NZ - 1)
+                def _():
+                    z_right(zl - step, h).start()
+
+                spread(zl - step, h)
+
+            @pl.when(zl + step < NZ)
+            def _(h=h):
+                z_left(zl + step, h).wait_recv()
+
+                @pl.when(zl > 0)
+                def _():
+                    z_left(zl + step, h).start()
+
+                spread(zl + step, h)
+
+        def pass_on(zs):
+            for h in order:
+                relay(zs, h)
+
+        both_sides(step - 1, pass_on)
+        both_sides(step - 2, forward)
+        both_sides(step - 4, collect)
+
+        @pl.when(step == COT_STEP)
+        def _():
+            for k in (0, 1):
+                for half in (0, 1):
+                    for n in range(3):
+                        cot_x(half, k, n).wait_recv()
+
+        first = jnp.where(step < COT_STEP, 0, jnp.where(step == COT_STEP, 0, step - 2))
+        last = jnp.where(step < COT_STEP, 0, step - 1)
+
+        @pl.loop(first, last)
+        def _(when):
+            both_sides(when, backward)
+
+    gsend[...] = acc[1 - c].astype(jnp.bfloat16)
+    g_sib = remote(gsend, grecv, sib_s.at[4], sib_r.at[4], sib)
+    g_sib.start()
+    for step in (NZ - 2, NZ - 1):
+        both_sides(jnp.int32(step), collect)
+    g_sib.wait()
+    g_ref[...] = acc[c] + grecv[...].astype(jnp.float32)
+
+    @pl.loop(0, NZ)
+    def _(zs):
+        for h in (0, 1):
+            y_plus(zs, y, h, 0).wait_send()
+            y_minus(zs, y, h, 1).wait_send()
+            y_plus(zs, y, h, 2).wait_send()
+
+            @pl.when((zs <= zl) & (zl < NZ - 1))
+            def _():
+                z_right(zs, h).wait_send()
+
+            @pl.when((zs >= zl) & (zl > 0))
+            def _():
+                z_left(zs, h).wait_send()
+
+        for n in range(3):
+            out_x(zs, n).wait_send()
+
+    for k in (0, 1):
+        for half in (0, 1):
+            for n in range(3):
+                cot_x(half, k, n).wait_send()
+
+
+COT_STEP = 5
+
+
+def project(weight, cot, cotz, gated):
+    rows = weight.shape[0]
+    dma = pltpu.SemaphoreType.DMA
+    vmem = pl.BlockSpec(memory_space=pltpu.VMEM)
+    toks = gated.shape[0]
+    return pl.pallas_call(
+        block_kernel,
+        out_shape=(
+            jax.ShapeDtypeStruct((toks, rows), jnp.float32),
+            jax.ShapeDtypeStruct((2, 2, NZ, 16, 512), jnp.bfloat16),
+        ),
+        in_specs=[vmem] * 4,
+        out_specs=(vmem, vmem),
+        scratch_shapes=[
+            pltpu.VMEM((NZ * NY, 2 * rows, 128), jnp.bfloat16),
+            pltpu.VMEM((4 * NX, NZ, 16, 512), jnp.bfloat16),
+            pltpu.VMEM((2, toks, rows), jnp.bfloat16),
+            pltpu.VMEM((2, toks, rows), jnp.float32),
+            pltpu.VMEM((NZ, NX, 2, 32, 512), jnp.bfloat16),
+            pltpu.VMEM((NZ, 3, 2, 32, 512), jnp.bfloat16),
+            pltpu.VMEM((toks, rows), jnp.bfloat16),
+            pltpu.VMEM((toks, rows), jnp.bfloat16),
+            dma((4,)), dma((5,)), dma((5,)),
+            dma((2, NZ, 2)), dma((NZ, 2)), dma((3, NZ, 2)), dma((3, NZ, 2)),
+            dma((2, 2, 3)), dma((2, 2, 3)), dma((NZ, 3)), dma((NZ, 3)),
+        ],
+        compiler_params=pltpu.CompilerParams(
+            collective_id=0, has_side_effects=True, vmem_limit_bytes=40 * 2**20
+        ),
+        name="project_both_ways",
+    )(weight, cot, cotz, gated)
+
+
+def sum_kernel(
+    f_ref, m_ref, o_ref, r_ref, mine, ybuf, zbuf, y_s, y_r, z_s, z_r, t_s, t_r, g_s, g_r, e_s, e_r, sib_s, sib_r
+):
+    ctx, tp, zl, y, zh, x, c = coords()
+    ys = [device(zl, (y + k) % NY, zh, x, c) for k in (1, 2, 3)]
+    zs = [device((zl + k) % NZ, y, zh, x, c) for k in range(1, NZ)]
+    sib = device(zl, y, zh, x, 1 - c)
+    greet([(sib, True)] + [(d, True) for d in ys + zs])
+    m_sib = remote(m_ref.at[1 - c], r_ref.at[c], sib_s, sib_r, sib)
+
+    def to_y(n):
+        return remote(f_ref.at[(y + n + 1) % NY], ybuf.at[n], y_s.at[n], y_r.at[n], ys[n])
+
+    def to_z(n):
+        return remote(mine.at[(zl + n + 1) % NZ], zbuf.at[n, 0], z_s.at[n], z_r.at[n], zs[n])
+
+    def taps_z(n):
+        return remote(mine.at[NZ], zbuf.at[n, 1], t_s.at[n], t_r.at[n], zs[n])
+
+    def back_z(n):
+        return remote(o_ref.at[y, zl], o_ref.at[y, zl], g_s.at[n], g_r.at[n], zs[n])
+
+    def back_y(n):
+        return remote(o_ref.at[y], o_ref.at[y], e_s.at[n], e_r.at[n], ys[n])
+
+    for n in range(3):
+        to_y(n).start()
+    m_sib.start()
+    r_ref[c] = m_ref[c]
+    value = f_ref[y].astype(jnp.float32)
+    for n in range(3):
+        to_y(n).wait_recv()
+        value = value + ybuf[n].astype(jnp.float32)
+    mine[...] = value.astype(jnp.bfloat16)
+    for n in range(NZ - 1):
+        to_z(n).start()
+        taps_z(n).start()
+    value = mine[zl].astype(jnp.float32)
+    taps = mine[NZ].astype(jnp.float32)
+    for n in range(NZ - 1):
+        to_z(n).wait_recv()
+        taps_z(n).wait_recv()
+        value = value + zbuf[n, 0].astype(jnp.float32)
+        taps = taps + zbuf[n, 1].astype(jnp.float32)
+    o_ref[y, zl] = value.astype(jnp.bfloat16)
+    o_ref[y, NZ] = taps.astype(jnp.bfloat16)
+    for n in range(NZ - 1):
+        back_z(n).start()
+    for n in range(NZ - 1):
+        back_z(n).wait()
+    for n in range(3):
+        back_y(n).start()
+    for n in range(3):
+        back_y(n).wait()
+    for n in range(3):
+        to_y(n).wait_send()
+    for n in range(NZ - 1):
+        to_z(n).wait_send()
+        taps_z(n).wait_send()
+    m_sib.wait()
+
+
+def sum_gradients(parts, mixed):
+    dma = pltpu.SemaphoreType.DMA
+    vmem = pl.BlockSpec(memory_space=pltpu.VMEM)
+    tile = parts.shape[1:]
+    return pl.pallas_call(
+        sum_kernel,
+        out_shape=(
+            jax.ShapeDtypeStruct(parts.shape, jnp.bfloat16),
+            jax.ShapeDtypeStruct(mixed.shape, jnp.bfloat16),
+        ),
+        in_specs=[vmem, vmem],
+        out_specs=(vmem, vmem),
+        scratch_shapes=[
+            pltpu.VMEM(tile, jnp.bfloat16),
+            pltpu.VMEM((3,) + tile, jnp.bfloat16),
+            pltpu.VMEM((NZ - 1, 2) + tile[1:], jnp.bfloat16),
+            dma((3,)), dma((3,)), dma((NZ - 1,)), dma((NZ - 1,)), dma((NZ - 1,)), dma((NZ - 1,)),
+            dma((NZ - 1,)), dma((NZ - 1,)), dma((3,)), dma((3,)), dma, dma,
+        ],
+        compiler_params=pltpu.CompilerParams(collective_id=2, has_side_effects=True),
+        name="sum_filter_gradients",
+    )(parts, mixed)
 
 
 def from_behind(value, axis, steps):
     count = lax.axis_size(axis)
     first, last = (max(0, -steps), min(count, count - steps))
     return lax.ppermute(value, axis, [(source, source + steps) for source in range(first, last)])
+
+
+def from_far(value):
+    count = lax.axis_size("tp")
+    return lax.ppermute(value, "tp", [(k, k ^ (count // 2)) for k in range(count)])
 
 
 def depthwise(signal, kernel):
@@ -38,6 +431,7 @@
     reach_len = long_pad + short_pad
     taps_flip = feat_taps[:, ::-1, :]
     filter_flip = long_filter[::-1]
+    zhalf = lax.axis_index("tp") // (2 * NX)
     tail_rows = jnp.concatenate(
         [
             branch_inputs[0, tok_count - short_pad :],
@@ -46,10 +440,17 @@
         ],
         axis=0,
     )
+    own_rows = cotangent.shape[0]
+    width = cotangent.shape[1]
+    cot_halves = jnp.pad(
+        cotangent.reshape(own_rows, NZ, NY, 2, 128).transpose(3, 1, 0, 2, 4).reshape(2, NZ, own_rows, 512),
+        ((0, 0), (0, 0), (0, 16 - own_rows), (0, 0)),
+    )
     arrived = from_behind(tail_rows, "ctx", 1)
+    cot_far = from_far(cot_halves)
     query_head = arrived[:short_pad]
     key_head = arrived[short_pad : short_pad + reach_len]
-    value_head = arrived[short_pad + reach_len :]
+    value_head = arrived[short_pad + reach_len : short_pad + 2 * reach_len]
     query_feat = featurize(
         jnp.concatenate([query_head, branch_inputs[0]], axis=0)[None], taps_flip[:1]
     )[0]
@@ -70,23 +471,13 @@
     long_sum = depthwise(pair_wide, filter_flip)
     query_wide = query_feat.astype(jnp.float32)
     gated_out = (query_wide * long_sum).astype(jnp.bfloat16)
-    whole_cotangent = lax.all_gather(cotangent, "tp", axis=0, tiled=True)
-    width_total = whole_cotangent.shape[1]
-    weight_piece = lax.all_gather(out_weight, "ctx", axis=1, tiled=True)
-    partial_out = jnp.zeros((tok_count, width_total), jnp.bfloat16)
-    product = jnp.dot(gated_out, weight_piece, preferred_element_type=jnp.float32).astype(
-        jnp.bfloat16
-    )
-    partial_out = lax.dynamic_update_slice_in_dim(partial_out, product, jnp.int32(0), 1)
-    grad_sum = lax.dot_general(
-        whole_cotangent, weight_piece, (((1,), (1,)), ((), ())), preferred_element_type=jnp.float32
-    )
-    partial_out, grad_mixed = (partial_out, grad_sum)
-    mixed_out = (
-        lax.psum_scatter(partial_out, "tp", scatter_dimension=0, tiled=True)
-        .astype(jnp.float32)
-        .astype(jnp.bfloat16)
-    )
+    gated_pad = jnp.pad(
+        gated_out.reshape(16, own_rows, chan_count), ((0, 0), (0, 16 - own_rows), (0, 0))
+    ).reshape(256, chan_count)
+    grad_pad, out_sums = project(out_weight, cot_halves, cot_far, gated_pad)
+    out_near = lax.dynamic_index_in_dim(out_sums, zhalf, 0, keepdims=False)
+    out_far = from_far(lax.dynamic_index_in_dim(out_sums, 1 - zhalf, 0, keepdims=False))
+    grad_mixed = grad_pad.reshape(16, 16, chan_count)[:, :own_rows].reshape(tok_count, chan_count)
     grad_long = grad_mixed * query_wide
     grad_query = grad_mixed * long_sum
     key_wide = key_feat.astype(jnp.float32)
@@ -114,10 +505,17 @@
     filter_part = depthwise(pair_wide, grad_long)[::-1]
     raw_full = jnp.concatenate([raw_heads, branch_inputs], axis=1).astype(jnp.float32)
     taps_part = jax.vmap(depthwise)(raw_full, grad_feat)[:, ::-1, :]
-    grad_filter, grad_taps = (
-        lax.psum(filter_part.astype(jnp.bfloat16), "ctx").astype(jnp.float32),
-        lax.psum(taps_part.astype(jnp.bfloat16), "ctx").astype(jnp.float32),
-    )
+    parts = jnp.concatenate(
+        [filter_part, taps_part.reshape(9, chan_count), jnp.zeros((7, chan_count), jnp.float32)], axis=0
+    ).astype(jnp.bfloat16)
+    mixed = (out_near.astype(jnp.float32) + out_far.astype(jnp.float32)).astype(jnp.bfloat16)
+    sums, mixed = sum_gradients(parts.reshape(9, 16, 4, 128).transpose(2, 0, 1, 3), mixed)
+    mixed_out = (
+        mixed[:, :, :own_rows].reshape(2, NZ, own_rows, NY, 128).transpose(2, 1, 3, 0, 4).reshape(own_rows, width)
+    )
+    sums = sums.transpose(1, 2, 0, 3).reshape(144, chan_count).astype(jnp.float32)
+    grad_filter = sums[:filter_len]
+    grad_taps = sums[filter_len : filter_len + 9].reshape(3, tap_count, chan_count)
     return (mixed_out, grad_in.astype(jnp.bfloat16), grad_filter, grad_taps)
 
 

time: 1090 us -> 227 us (0.21)
  waiting for transfers between devices: 636 us -> 0.01 us
  blocking collectives: 319 us -> 0 us
  Pallas kernels: 0 us -> 133 us
  starting transfers between devices: 43.5 us -> 29.9 us
  between operations: 15 us -> 1.47 us
    psum x1 -> x0, waiting for transfers between devices: 325 us -> none  [body(): lax.psum(filter_part.astype(jnp.bfloat16), 'ctx').astype(jnp.float32)]
    all_gather x2 -> x0, waiting for transfers between devices: 307 us -> none  [the longest x1 205 us: body(): weight_piece = lax.all_gather(out_weight, 'ctx', axis=1, tiled=True)]
    psum x1 -> x0, blocking collectives: 232 us -> none  [body(): lax.psum(taps_part.astype(jnp.bfloat16), 'ctx').astype(jnp.float32)]
    pallas_call x0 -> x2, Pallas kernels: none -> 133 us  [the longest x1 89.3 us: project(): pl.pallas_call(block_kernel, out_shape=(jax.ShapeDtypeStruct((toks, rows)...]
    unnamed x1 -> x0, blocking collectives: 86.7 us -> none
    unnamed x4 -> x0, starting transfers between devices: 38.4 us -> none
    ppermute x0 -> x2, starting transfers between devices: none -> 24.8 us  [from_far(): lax.ppermute(value, 'tp', [(k, k ^ count // 2) for k in range(count)])]
    dot_general x2 -> x0, matrix products: 12.7 us -> none  [the longest x1 7.28 us: body(): lax.dot_general(whole_cotangent, weight_piece, (((1,), (1,)), ((), ())),...]
  transfers between devices with their start and end apart: 9 -> 4, of which waited for: 4 -> 0; matrix products, arithmetic and copies ran while one was open for 13% -> 20% of each run, Pallas kernels for 0% -> 0%
where the time goes in v2:
time: 227 us; the launch traced here: 226 us
  Pallas kernels  133 us (59%)
  starting transfers between devices  29.9 us (13%)
  local copies, waits for them, and re-layouts  28.4 us (13%)
  matrix products  26.4 us (12%)
  other arithmetic  6.85 us (3%)
    pallas_call x1, Pallas kernels, project(): pl.pallas_call(block_kernel, out_shape=(jax.ShapeDtypeStruct((toks, rows)...  89.3 us
    pallas_call x1, Pallas kernels, sum_gradients(): pl.pallas_call(sum_kernel, out_shape=(jax.ShapeDtypeStruct(parts.shape, j...  43.2 us
    conv_general_dilated x8, matrix products, depthwise(): lax.conv_general_dilated(signal[None], kernel[:, None, :], (1,), 'VALID',...  26.4 us
    ppermute x2, starting transfers between devices, from_far(): lax.ppermute(value, 'tp', [(k, k ^ count // 2) for k in range(count)])  24.8 us
    reshape x10, local copies, waits for them, and re-layouts, depthwise(): lax.conv_general_dilated(signal[None], kernel[:, None, :], (1,), 'VALID',...  9.36 us
    ppermute x2, starting transfers between devices, from_behind(): lax.ppermute(value, axis, [(source, source + steps) for source in range(f...  5.1 us
  transfers between devices with their start and end apart: 4, of which 0 were waited for; matrix products, arithmetic and copies ran while one was open for 20% of the time, Pallas kernels for 0%

profile of v2, /device:TPU:6, one launch (start us, length us, event | category | flops | bytes accessed | tf_op | source)
XLA Modules:
  0.0 225.6 jit_solution(4339753513515544335)
XLA Ops:
  0.6 0.7 slice_bitcast_fusion.8
  1.4 1.0 slice_bitcast_fusion.5
  2.6 3.6 %collective-permute-start = (bf16[260,512]{1,0:T(8,128)(2,1)S(1)}, bf16[260,512]{1,0:T(8,128)(2,1)S(1)}, u32[]{:S(2)}, u32[]{:S(2)}) collective-permute-start(bf16[260,512]{1,0:T(8,128)(2,1)S(1)} %pad_maximum_fusion), channel_id=1, source_target_pairs={{0,16},{16,32},{32,48},{48,64},{64,80},{80,96},{96,112},{112,128},... | collective-permute-start | bytes 798728 | tf_op jit(solution)/shard_map/ppermute | solution.py:398
  6.2 0.1 reshape.145
  6.5 15.7 %collective-permute-start.1 = (bf16[2,8,16,512]{3,2,1,0:T(8,128)(2,1)S(1)}, bf16[2,8,16,512]{3,2,1,0:T(8,128)(2,1)S(1)}, u32[]{:S(2)}, u32[]{:S(2)}) collective-permute-start(bf16[2,8,16,512]{3,2,1,0:T(8,128)(2,1)S(1)} %pad.8.cot_ref), channel_id=1, source_target_pairs={{0,8},{1,9},{2,10},{3,11},{4,12},{5,13},{6,14},{7,15},{8,0},{9,1},... | collective-permute-start | bytes 786440 | tf_op jit(solution)/shard_map/ppermute | solution.py:403
  22.3 0.1 slice.123
  22.4 0.1 slice.117
  22.6 1.3 rev.10
  24.1 0.1 maximum_bitcast_fusion.5
  24.3 0.5 copy.63
  24.8 1.9 reshape.179
  26.7 6.0 %fusion.6 = bf16[319,1024]{1,0:T(8,128)(2,1)S(1)} fusion(bf16[1,321,1024]{2,0,1:T(2,128)(2,1)} %reshape.179, bf16[3,1,1024]{2,0,1:T(4,128)(2,1)S(1)} %bitcast.151), kind=kOutput, calls=%fused_computation.13 | convolution fusion | flops 2286592 | bytes 1316864 | tf_op jit(solution)/shard_map/vmap()/conv_general_dilated | solution.py:407
  32.7 0.4 convert_element_type.121
  33.2 0.8 copy-done.19
  34.0 4.1 %fusion.12 = f32[1,192,512]{2,0,1:T(1,128)S(1)} fusion(bf16[1,319,512]{2,1,0:T(8,128)(2,1)S(1)} %fusion.17, f32[128,1,512]{2,0,1:T(8,128)S(1)} %bitcast.147), kind=kOutput, calls=%fused_computation.26 | convolution fusion | flops 150994944 | bytes 982016 | tf_op jit(solution)/shard_map/conv_general_dilated | solution.py:407
  38.2 1.7 convert_reduce_fusion
  40.1 89.3 %project_both_ways.1 = (f32[256,512]{1,0:T(8,128)S(1)}, bf16[2,2,8,16,512]{4,3,2,1,0:T(8,128)(2,1)S(1)}) custom-call(bf16[512,256]{1,0:T(8,128)(2,1)S(1)} %copy-done, bf16[2,8,16,512]{3,2,1,0:T(8,128)(2,1)S(1)} %pad.8.cot_ref, bf16[2,8,16,512]{3,2,1,0:T(8,128)(2,1)S(1)} %collective-permute-done.1.cotz_ref, bf16[256,512]{1,0:T(8,128)(2,1)S(1)} %bitcast.131), custom_call_target="tpu_custom_call" | custom-call | tf_op jit(solution)/shard_map/project_both_ways/pallas_call | solution.py:281
  129.4 1.1 bitcast_multiply_fusion
  130.4 0.7 slice.193
  131.1 0.7 slice_bitcast_fusion
  131.8 0.8 reshape.152
  132.7 1.2 reshape.180
  133.9 0.1 maximum_bitcast_fusion.4
  134.0 0.4 copy.75
  134.5 1.4 reshape.181
  135.9 0.7 dynamic-slice_bitcast_fusion
  136.6 9.1 %collective-permute-start.3 = (bf16[2,8,16,512]{3,2,1,0:T(8,128)(2,1)}, bf16[2,8,16,512]{3,2,1,0:T(8,128)(2,1)}, u32[]{:S(2)}, u32[]{:S(2)}) collective-permute-start(bf16[2,8,16,512]{3,2,1,0:T(8,128)(2,1)} %dynamic-slice_bitcast_fusion), channel_id=1, source_target_pairs={{0,8},{1,9},{2,10},{3,11},{4,12},{5,13},{6,14},{7,15},{8,0},{9,1},... | collective-permute-start | bytes 786440 | tf_op jit(solution)/shard_map/ppermute | solution.py:403
  145.7 1.1 copy_multiply_fusion
  146.8 0.7 fusion.18
  147.5 0.1 copy-done.7
  147.7 1.5 collective-permute-start.2
  149.2 5.6 %fusion.14 = bf16[1,128,512]{2,0,1:T(2,128)(2,1)S(1)} fusion(bf16[1,319,512]{2,1,0:T(8,128)(2,1)S(1)} %copy-done.12, f32[192,1,512]{2,1,0:T(1,128)S(1)} %copy-done.8, f32[1,192,512]{2,0,1:T(1,128)S(1)} %copy-done.9), kind=kOutput, calls=%fused_computation.28 | convolution fusion | flops 151093248 | bytes 1244160 | tf_op jit(solution)/shard_map/conv_general_dilated | solution.py:407
  154.8 0.2 rev.11
  155.1 0.6 copy-done.18
  155.7 4.1 %fusion.9 = f32[1,192,512]{2,0,1:T(1,128)S(1)} fusion(f32[1,319,512]{2,1,0:T(8,128)S(1)} %maximum_bitcast_fusion.3, f32[128,1,512]{2,0,1:T(8,128)S(1)} %bitcast.146), kind=kOutput, calls=%fused_computation.19 | convolution fusion | flops 150994944 | bytes 1308672 | tf_op jit(solution)/shard_map/conv_general_dilated | solution.py:407
  159.9 0.1 convert_multiply_fusion.1
  160.0 1.1 maximum_bitcast_fusion.1
  161.1 0.1 maximum_bitcast_fusion
  161.2 0.8 copy.92
  162.0 0.9 reshape.162
  162.9 0.1 pad.10
  163.0 1.5 reshape.168
  164.6 1.0 copy-done.4
  165.6 0.7 slice.162
  166.3 0.8 copy.85
  167.1 2.5 %reshape.182 = f32[192,1,1536]{2,1,0:T(1,128)} reshape(f32[192,1,3,512]{3,2,0,1:T(4,128)S(1)} %copy.85) | data formatting | bytes 2359296 | tf_op jit(solution)/shard_map/vmap()/reshape | solution.py:407
  169.7 3.9 %convolution_reduce_fusion = bf16[3,1536]{1,0:T(4,128)(2,1)S(1)} fusion(bf16[1,194,1536]{2,0,1:T(2,128)(2,1)S(1)} %copy-done.6, f32[192,1,1536]{2,1,0:T(1,128)} %reshape.182), kind=kOutput, calls=%fused_computation.12 | convolution fusion | flops 10616832 | bytes 1784832 | tf_op jit(solution)/shard_map/vmap()/conv_general_dilated | solution.py:407
  173.6 0.3 fusion
  174.0 0.2 copy.96
  174.2 0.2 reshape.172
  174.4 0.4 convert_element_type.145
  174.9 0.9 copy.99
  175.9 0.1 maximum_maximum_fusion
  176.0 0.7 copy.158
  176.7 1.7 fusion.11.m_ref
  178.5 43.2 %sum_filter_gradients.1 = (bf16[4,9,16,128]{3,2,1,0:T(8,128)(2,1)}, bf16[2,8,16,512]{3,2,1,0:T(8,128)(2,1)}) custom-call(bf16[4,9,16,128]{3,2,1,0:T(8,128)(2,1)} %bitcast.141, bf16[2,8,16,512]{3,2,1,0:T(8,128)(2,1)} %fusion.11.m_ref), custom_call_target="tpu_custom_call" | custom-call | tf_op jit(solution)/shard_map/sum_filter_gradients/pallas_call | solution.py:375
  221.7 1.0 convert_bitcast_fusion
  222.7 0.1 copy.98
  222.9 0.1 copy.156
  223.0 0.2 copy.91
  223.2 0.8 reshape.159
  224.1 0.6 reshape.165
  224.7 0.2 copy.97
  224.9 0.7 copy.154
  (84 shorter events, 1.3 us)
Async XLA Ops:
  0.6 5.6 %copy-start.14 = (bf16[12,8192]{1,0:T(8,128)(2,1)S(1)}, bf16[12,8192]{1,0:T(8,128)(2,1)}, u32[]{:S(2)}) copy-start(bf16[12,8192]{1,0:T(8,128)(2,1)} %param.9) | copy-start | bytes 589828
  2.4 19.8 %slice-start = ((bf16[3,3,512]{2,1,0:T(4,128)(2,1)}), bf16[1,3,512]{2,1,0:T(4,128)(2,1)S(1)}, s32[]{:S(2)}) async-start(bf16[3,3,512]{2,1,0:T(4,128)(2,1)} %param.6), calls=%async_computation | async-start | bytes 8192 | tf_op jit(solution)/shard_map/slice | solution.py:455
  2.4 20.0 %slice-start.1 = ((bf16[3,3,512]{2,1,0:T(4,128)(2,1)}), bf16[2,3,512]{2,1,0:T(4,128)(2,1)S(1)}, s32[]{:S(2)}) async-start(bf16[3,3,512]{2,1,0:T(4,128)(2,1)} %param.6), calls=%async_computation.1 | async-start | bytes 16384 | tf_op jit(solution)/shard_map/slice | solution.py:463
  2.5 20.1 %copy-start.16 = (f32[128,512]{1,0:T(8,128)S(1)}, f32[128,512]{1,0:T(8,128)}, u32[]{:S(2)}) copy-start(f32[128,512]{1,0:T(8,128)} %param.7) | copy-start | bytes 786436
  2.5 21.4 %copy-start.2 = (bf16[3,192,512]{2,1,0:T(8,128)(2,1)S(1)}, bf16[3,192,512]{2,1,0:T(8,128)(2,1)}, u32[]{:S(2)}) copy-start(bf16[3,192,512]{2,1,0:T(8,128)(2,1)} %param.5) | copy-start | bytes 1769476
  2.6 21.5 %collective-permute-start = (bf16[260,512]{1,0:T(8,128)(2,1)S(1)}, bf16[260,512]{1,0:T(8,128)(2,1)S(1)}, u32[]{:S(2)}, u32[]{:S(2)}) collective-permute-start(bf16[260,512]{1,0:T(8,128)(2,1)S(1)} %pad_maximum_fusion), channel_id=1, source_target_pairs={{0,16},{16,32},{32,48},{48,64},{64,80},{80,96},{96,112},{112,128},... | collective-permute-start | bytes 798728 | tf_op jit(solution)/shard_map/ppermute | solution.py:398
  6.5 33.5 %collective-permute-start.1 = (bf16[2,8,16,512]{3,2,1,0:T(8,128)(2,1)S(1)}, bf16[2,8,16,512]{3,2,1,0:T(8,128)(2,1)S(1)}, u32[]{:S(2)}, u32[]{:S(2)}) collective-permute-start(bf16[2,8,16,512]{3,2,1,0:T(8,128)(2,1)S(1)} %pad.8.cot_ref), channel_id=1, source_target_pairs={{0,8},{1,9},{2,10},{3,11},{4,12},{5,13},{6,14},{7,15},{8,0},{9,1},... | collective-permute-start | bytes 786440 | tf_op jit(solution)/shard_map/ppermute | solution.py:403
  33.0 1.0 copy-start.19
  33.2 4.9 %copy-start.11 = (bf16[1,319,512]{2,1,0:T(8,128)(2,1)}, bf16[1,319,512]{2,1,0:T(8,128)(2,1)S(1)}, u32[]{:S(2)}) copy-start(bf16[1,319,512]{2,1,0:T(8,128)(2,1)S(1)} %fusion.17) | copy-start | bytes 979972
  38.1 1.8 copy-start.10
  38.2 1.8 copy-start
  134.4 11.2 %copy-start.3 = (f32[1,192,512]{2,1,0:T(8,128)S(1)}, f32[1,192,512]{2,1,0:T(8,128)}, u32[]{:S(2)}) copy-start(f32[1,192,512]{2,1,0:T(8,128)} %reshape.152) | copy-start | bytes 1179652
  135.9 10.9 %copy-start.13 = (f32[1,129,512]{2,1,0:T(8,128)S(1)}, f32[1,129,512]{2,1,0:T(8,128)}, u32[]{:S(2)}) copy-start(f32[1,129,512]{2,1,0:T(8,128)} %slice_bitcast_fusion) | copy-start | bytes 792580
  135.9 10.9 %copy-start.17 = (f32[128,512]{1,0:T(8,128)S(1)}, f32[128,512]{1,0:T(8,128)}, u32[]{:S(2)}) copy-start(f32[128,512]{1,0:T(8,128)} %param.7) | copy-start | bytes 786436
  136.6 40.1 %collective-permute-start.3 = (bf16[2,8,16,512]{3,2,1,0:T(8,128)(2,1)}, bf16[2,8,16,512]{3,2,1,0:T(8,128)(2,1)}, u32[]{:S(2)}, u32[]{:S(2)}) collective-permute-start(bf16[2,8,16,512]{3,2,1,0:T(8,128)(2,1)} %dynamic-slice_bitcast_fusion), channel_id=1, source_target_pairs={{0,8},{1,9},{2,10},{3,11},{4,12},{5,13},{6,14},{7,15},{8,0},{9,1},... | collective-permute-start | bytes 786440 | tf_op jit(solution)/shard_map/ppermute | solution.py:403
  146.7 0.9 copy-start.7
  146.8 2.4 %copy-start.8 = (f32[192,1,512]{2,1,0:T(1,128)S(1)}, f32[192,1,512]{2,1,0:T(1,128)}, u32[]{:S(2)}) copy-start(f32[192,1,512]{2,1,0:T(1,128)} %reshape.180) | copy-start | bytes 1179652
  146.8 2.4 %copy-start.9 = (f32[1,192,512]{2,0,1:T(1,128)S(1)}, f32[1,192,512]{2,0,1:T(1,128)}, u32[]{:S(2)}) copy-start(f32[1,192,512]{2,0,1:T(1,128)} %get-tuple-element.40) | copy-start | bytes 1179652
  146.8 2.4 %copy-start.12 = (bf16[1,319,512]{2,1,0:T(8,128)(2,1)S(1)}, bf16[1,319,512]{2,1,0:T(8,128)(2,1)}, u32[]{:S(2)}) copy-start(bf16[1,319,512]{2,1,0:T(8,128)(2,1)} %copy-done.11) | copy-start | bytes 979972
  147.7 7.3 %collective-permute-start.2 = (bf16[133,512]{1,0:T(8,128)(2,1)S(1)}, bf16[133,512]{1,0:T(8,128)(2,1)S(1)}, u32[]{:S(2)}, u32[]{:S(2)}) collective-permute-start(bf16[133,512]{1,0:T(8,128)(2,1)S(1)} %pad_maximum_fusion.1), channel_id=1, source_target_pairs={{16,0},{32,16},{48,32},{64,48},{80,64},{96,80},{112,96},{128,112},... | collective-permute-start | bytes 408584 | tf_op jit(solution)/shard_map/ppermute | solution.py:398
  154.8 1.0 copy-start.18
  164.5 1.8 copy-start.1
  164.6 1.0 copy-start.4
  167.1 2.5 %copy-start.6 = (bf16[1,194,1536]{2,0,1:T(2,128)(2,1)S(1)}, bf16[1,194,1536]{2,0,1:T(2,128)(2,1)}, u32[]{:S(2)}) copy-start(bf16[1,194,1536]{2,0,1:T(2,128)(2,1)} %reshape.181) | copy-start | bytes 1787908
  169.6 4.0 %copy-start.5 = (f32[1,8,25,1536]{3,1,2,0:T(8,128)S(1)}, f32[1,8,25,1536]{3,1,2,0:T(8,128)}, u32[]{:S(2)}) copy-start(f32[1,8,25,1536]{3,1,2,0:T(8,128)} %copy-done.4) | copy-start | bytes 3686404
  169.6 4.0 %copy-start.20 = (f32[1,7,2,1536]{3,1,2,0:T(8,128)S(1)}, f32[1,7,2,1536]{3,1,2,0:T(8,128)}, u32[]{:S(2)}) copy-start(f32[1,7,2,1536]{3,1,2,0:T(8,128)} %slice.162) | copy-start | bytes 258052
  169.6 4.0 %copy-start.21 = (bf16[3,3,512]{2,1,0:T(4,128)(2,1)S(1)}, bf16[3,3,512]{2,1,0:T(4,128)(2,1)}, u32[]{:S(2)}) copy-start(bf16[3,3,512]{2,1,0:T(4,128)(2,1)} %param.6) | copy-start | bytes 27652
  169.6 4.0 %copy-start.22 = (pred[8,25]{0,1:T(8,128)(4,1)S(1)}, pred[8,25]{0,1:T(8,128)(4,1)}, u32[]{:S(2)}) copy-start(pred[8,25]{0,1:T(8,128)(4,1)} %constant.59) | copy-start | bytes 604
  221.7 1.1 copy-start.15

commit v3 on v2

v3 whole, which is shorter than its diff:
```python
import functools

import jax
import jax.numpy as jnp
from jax import lax
from jax.experimental import pallas as pl
from jax.experimental.pallas import tpu as pltpu
from jax.sharding import PartitionSpec as P

MESH = pl.DeviceIdType.MESH
NZ, NY, NX = 8, 4, 4


def coords():
    ctx = lax.axis_index("ctx")
    tp = lax.axis_index("tp")
    return ctx, tp, ctx // NY, ctx % NY, tp // (2 * NX), (tp // 2) % NX, tp % 2


def device(zl, y, zh, x, c):
    return {"ctx": zl * NY + y, "tp": zh * (2 * NX) + x * 2 + c}


def remote(src, dst, send, recv, target):
    return pltpu.make_async_remote_copy(
        src_ref=src, dst_ref=dst, send_sem=send, recv_sem=recv, device_id=target, device_id_type=MESH
    )


def greet(targets):
    barrier = pltpu.get_barrier_semaphore()
    count = 0
    for target, there in targets:
        if there is True:
            pl.semaphore_signal(barrier, inc=1, device_id=target, device_id_type=MESH)
            count = count + 1
        else:
            @pl.when(there)
            def _():
                pl.semaphore_signal(barrier, inc=1, device_id=target, device_id_type=MESH)

            count = count + there.astype(jnp.int32)
    pl.semaphore_wait(barrier, count)


T = 192
PRE = 144
TAIL = 16
F32, BF16 = jnp.float32, jnp.bfloat16


def block_kernel(
    br_ref, taps_ref, fil_ref, w_ref, cot_ref,
    mixed_ref, gin_ref, gfil_ref, gtap_ref,
    wg, cp, cg, halo, qf, kf, vf, ls, rot, gated, both, acc, out, arrived, gsend, grecv,
    sums, far, near, come, other, glb, rg, gq, gk, gv, head, head_in, lead, lead_in, tg,
    part, mine, ybuf, zbuf, total, tpart, tmine, tybuf, tzbuf,
    own_sem, sib_s, sib_r, z_s, z_r, y_s, y_r, x_s, x_r, o_s, o_r, zp_s, zp_r, h_s, h_r,
    py_s, py_r, pz_s, pz_r, pt_s, pt_r, bz_s, bz_r, by_s, by_r, ty_s, ty_r,
):
    ctx, tp, zl, y, zh, x, c = coords()
    yp = device(zl, (y + 1) % NY, zh, x, c)
    ym = device(zl, (y + 3) % NY, zh, x, c)
    sib = device(zl, y, zh, x, 1 - c)
    zpart = device(zl, y, 1 - zh, x, c)
    xs = [device(zl, y, zh, (x + k) % NX, c) for k in (1, 2, 3)]
    ys = [device(zl, (y + k) % NY, zh, x, c) for k in (1, 2, 3)]
    zs_all = [device((zl + k) % NZ, y, zh, x, c) for k in range(1, NZ)]
    dright = device(jnp.minimum(zl + 1, NZ - 1), y, zh, x, c)
    dleft = device(jnp.maximum(zl - 1, 0), y, zh, x, c)
    last_ctx = NZ * NY - 1
    nxt = {"ctx": jnp.minimum(ctx + 1, last_ctx), "tp": tp}
    prv = {"ctx": jnp.maximum(ctx - 1, 0), "tp": tp}
    greet(
        [(sib, True), (zpart, True)]
        + [(d, True) for d in xs + ys + zs_all]
        + [(nxt, ctx < last_ctx), (prv, ctx > 0)]
    )
    rows = w_ref.shape[0]

    def unit(zs, yy, h):
        return wg.at[zs * NY + yy, pl.ds(pl.multiple_of(h * rows, rows), rows)]

    keep = w_ref.at[:, pl.ds(pl.multiple_of(c * 128, 128), 128)]
    give = w_ref.at[:, pl.ds(pl.multiple_of((1 - c) * 128, 128), 128)]
    w_sib = remote(give, unit(zl, y, c), sib_s.at[0], sib_r.at[0], sib)
    w_sib.start()
    w_own = pltpu.make_async_copy(keep, unit(zl, y, c), own_sem.at[0])
    w_own.start()
    c_sib = remote(cot_ref.at[1 - c], cp.at[tp], sib_s.at[1], sib_r.at[1], sib)
    c_sib.start()
    c_own = pltpu.make_async_copy(cot_ref.at[c], cp.at[tp], own_sem.at[1])
    c_own.start()
    halo_copies = [
        remote(br_ref.at[b, pl.ds(T - n, n)], halo.at[pl.ds(at, n)], h_s.at[b], h_r.at[b], nxt)
        for b, n, at in ((0, TAIL, 0), (1, PRE, TAIL), (2, PRE, TAIL + PRE))
    ]

    @pl.when(ctx < last_ctx)
    def _():
        for copy in halo_copies:
            copy.start()

    def z_right(zs, h):
        return remote(unit(zs, y, h), unit(zs, y, h), z_s.at[0, zs, h], z_r.at[zs, h], dright)

    def z_left(zs, h):
        return remote(unit(zs, y, h), unit(zs, y, h), z_s.at[1, zs, h], z_r.at[zs, h], dleft)

    def y_plus(zs, yy, h, kind):
        return remote(unit(zs, yy, h), unit(zs, yy, h), y_s.at[kind, zs, h], y_r.at[kind, zs, h], yp)

    def y_minus(zs, yy, h, kind):
        return remote(unit(zs, yy, h), unit(zs, yy, h), y_s.at[kind, zs, h], y_r.at[kind, zs, h], ym)

    def spread(zs, h):
        y_plus(zs, y, h, 0).start()
        y_minus(zs, y, h, 1).start()

    def relay(zs, h):
        y_plus(zs, (y + 3) % NY, h, 0).wait_recv()
        y_minus(zs, (y + 1) % NY, h, 1).wait_recv()

        @pl.when(h == 0)
        def _():
            y_plus(zs, (y + 3) % NY, h, 2).start()

        @pl.when(h == 1)
        def _():
            y_minus(zs, (y + 1) % NY, h, 2).start()

    def cot_z(k):
        piece = zh * (2 * NX) + x * 2 + k
        return remote(cp.at[piece], cp.at[piece], zp_s.at[k], zp_r.at[k], zpart)

    def cot_x(half, k, n):
        piece = half * (2 * NX) + x * 2 + k
        return remote(cp.at[piece], cp.at[piece], x_s.at[half, k, n], x_r.at[half, k, n], xs[n])

    def out_x(zs, n):
        return remote(out.at[zs, (x + n + 1) % NX], arrived.at[zs, n], o_s.at[zs, n], o_r.at[zs, n], xs[n])

    order = (c, 1 - c)
    w_own.wait()
    for h in order:
        if h is not c:
            w_sib.wait()

        @pl.when(zl < NZ - 1)
        def _(h=h):
            z_right(zl, h).start()

        @pl.when(zl > 0)
        def _(h=h):
            z_left(zl, h).start()

        spread(zl, h)
        if h is c:
            c_own.wait()
        else:
            c_sib.wait()
        cot_z(h).start()
        for n in range(3):
            cot_x(zh, h, n).start()
    acc[...] = jnp.zeros_like(acc)
    tg[...] = jnp.zeros_like(tg)

    @pl.when(ctx == 0)
    def _():
        halo[...] = jnp.zeros_like(halo)

    @pl.when(ctx == last_ctx)
    def _():
        head_in[...] = jnp.zeros_like(head_in)
        lead_in[...] = jnp.zeros_like(lead_in)

    def lane(l):
        return pl.ds(pl.multiple_of(l * 128, 128), 128)

    def spaced(value, count):
        shifted = pltpu.roll(value, value.shape[0] - 4, 0)
        for i in range(count):
            at = 12 * i
            yield (value[at : at + 16] if at % 8 == 0 else shifted[at - 4 : at + 12]).astype(BF16)

    def convolve(source, first, step, lanes):
        def residue(r, value):
            for q in range(16):
                tap = fil_ref[r, q : q + 1, lanes]
                value = value + tap * source(r, first + step * 8 * q)
            return value

        return lax.fori_loop(0, 8, residue, jnp.zeros((T, 128), F32))

    def features(l):
        lanes = lane(l)

        def feature(b, at, n):
            raw = jnp.concatenate([halo[at : at + n, lanes].astype(F32), br_ref[b, :, lanes].astype(F32)], axis=0)
            value = taps_ref[3 * b : 3 * b + 1, lanes] * raw
            for i in (1, 2):
                value = value + taps_ref[3 * b + i : 3 * b + i + 1, lanes] * pltpu.roll(raw, i, 0)
            return value.astype(BF16).astype(F32)

        query = feature(0, 0, TAIL)[TAIL:]
        key = feature(1, TAIL, PRE)
        value = feature(2, TAIL + PRE, PRE)
        qf[:, lanes] = query
        kf[:, lanes] = key[PRE:]
        vf[:, lanes] = value[PRE:]
        pair = (key * value).astype(BF16).astype(F32)
        rot[0, :, lanes] = pair
        for r in range(1, 8):
            rot[r, :, lanes] = pltpu.roll(pair, r, 0)
        long = convolve(lambda r, at: rot[r, pl.ds(at, T), lanes], PRE, -1, lanes)
        ls[:, lanes] = long
        for i, rows16 in enumerate(spaced(query * long, 16)):
            gated[16 * i : 16 * i + 16, lanes] = rows16

    def weight(zs, k):
        return jnp.concatenate([wg[zs * NY + yy, k * rows : (k + 1) * rows] for yy in range(NY)], axis=1)

    def forward(zs):
        value = jnp.dot(both[0], weight(zs, 0), preferred_element_type=F32)
        value = value + jnp.dot(both[1], weight(zs, 1), preferred_element_type=F32)
        value = value.astype(BF16)
        for half in (0, 1):
            for xx in range(NX):
                at = (half * NX + xx) * 32
                out[zs, xx, half] = value[at : at + 32]
        for n in range(3):
            out_x(zs, n).start()

    def backward(zs):
        for k in (0, 1):
            acc[k] += lax.dot_general(
                cg[zs], weight(zs, k), (((1,), (1,)), ((), ())), preferred_element_type=F32
            )

    def collect(zs):
        value = out[zs, x].astype(F32)
        for n in range(3):
            out_x(zs, n).wait_recv()
            value = value + arrived[zs, n].astype(F32)
        value = value.astype(BF16)
        for half in (0, 1):
            for k in (0, 1):
                sums[half, k, zs] = value[half, k * 16 : (k + 1) * 16]

    def both_sides(step, act):
        @pl.loop(0, 2)
        def _(side):
            zs = zl + (2 * side - 1) * step

            @pl.when((step >= 0) & (zs >= 0) & (zs < NZ) & ((step > 0) | (side == 0)))
            def _():
                act(zs)

    x_sib = remote(gated, both.at[c], sib_s.at[2], sib_r.at[2], sib)
    x_own = pltpu.make_async_copy(gated, both.at[c], own_sem.at[2])

    def forward_done(step):
        return jnp.maximum(0, jnp.minimum(2 * (step - 4), step - 1))

    def backward_done(step):
        return jnp.maximum(0, jnp.minimum(3 * (step - 5), step - 1))

    @pl.loop(1, NZ + 2)
    def _(step):
        for h in order:
            @pl.when((zl - step >= 0) & (step < NZ))
            def _(h=h):
                z_right(zl - step, h).wait_recv()

                @pl.when(zl < NZ - 1)
                def _():
                    z_right(zl - step, h).start()

                spread(zl - step, h)

            @pl.when(zl + step < NZ)
            def _(h=h):
                z_left(zl + step, h).wait_recv()

                @pl.when(zl > 0)
                def _():
                    z_left(zl + step, h).start()

                spread(zl + step, h)

        def pass_on(zs):
            for h in order:
                relay(zs, h)

        def relayed(zs):
            for h in (0, 1):
                y_plus(zs, (y + 2) % NY, h, 2).wait_recv()

        both_sides(step - 1, pass_on)
        both_sides(step - 2, relayed)

        @pl.when((step == 1) & (ctx > 0))
        def _():
            for copy in halo_copies:
                copy.wait_recv()

        @pl.when(step <= 4)
        def _():
            features(step - 1)

        @pl.when(step == 4)
        def _():
            x_sib.start()
            x_own.start()
            for k in order:
                cot_z(k).wait_recv()
                for n in range(3):
                    cot_x(1 - zh, k, n).start()

        @pl.when(step == 5)
        def _():
            x_own.wait()
            x_sib.wait()

        @pl.when(step == 6)
        def _():
            for k in (0, 1):
                for half in (0, 1):
                    for n in range(3):
                        cot_x(half, k, n).wait_recv()

            @pl.loop(0, 4 * NX)
            def _(piece):
                at = pl.ds(pl.multiple_of(piece * 16, 16), 16)
                for zs, rows16 in enumerate(spaced(cp[piece].astype(F32), NZ)):
                    cg[zs, at] = rows16

        @pl.loop(forward_done(step - 1), forward_done(step))
        def _(when):
            both_sides(when, forward)

        @pl.loop(backward_done(step - 1), backward_done(step))
        def _(when):
            both_sides(when, backward)

        @pl.loop(forward_done(step - 2), forward_done(step - 1))
        def _(when):
            both_sides(when, collect)

    gsend[...] = acc[1 - c].astype(BF16)
    g_sib = remote(gsend, grecv, sib_s.at[3], sib_r.at[3], sib)
    g_sib.start()
    both_sides(jnp.int32(NZ - 1), collect)
    out_far = remote(sums.at[1 - zh], far, zp_s.at[2], zp_r.at[2], zpart)
    out_far.start()
    g_sib.wait()

    def gradients(l):
        lanes = lane(l)
        low = lax.broadcasted_iota(jnp.int32, (8, 128), 0) < 4
        tiles = []
        for m in range(8):
            at = 32 * m
            block = acc[c, at : at + 32, lanes] + grecv[at : at + 32, lanes].astype(F32)
            up, down = pltpu.roll(block[16:24], 4, 0), pltpu.roll(block[24:32], 4, 0)
            tiles += [block[:8], jnp.where(low, block[8:16], up), jnp.where(low, up, down)]
        mixed_grad = jnp.concatenate(tiles, axis=0)
        long_grad = mixed_grad * qf[:, lanes]
        query_grad = mixed_grad * ls[:, lanes]
        glb[:T, lanes] = long_grad
        gq[:, lanes] = query_grad
        head[:128, lanes] = long_grad[:128].astype(BF16)
        head[128:, lanes] = query_grad[:TAIL].astype(BF16)

    @pl.loop(0, 4)
    def _(l):
        gradients(l)

    head_copy = remote(head, head_in, h_s.at[3], h_r.at[3], prv)

    @pl.when(ctx > 0)
    def _():
        head_copy.start()

    @pl.loop(0, 4)
    def _(l):
        lanes = lane(l)
        grad = glb[:T, lanes]

        @pl.loop(0, 8)
        def _(r):
            for q in range(16):
                total[r, q : q + 1, lanes] = jnp.sum(
                    grad * rot[r, pl.ds(PRE - 8 * q, T), lanes], axis=0, keepdims=True
                )

        for t in range(8):
            part[l, t] = total[t, :, lanes].astype(BF16)

    def to_y(n):
        return remote(part.at[(y + n + 1) % NY], ybuf.at[n], py_s.at[n], py_r.at[n], ys[n])

    def taps_y(n):
        return remote(tpart.at[(y + n + 1) % NY], tybuf.at[n], ty_s.at[n], ty_r.at[n], ys[n])

    def to_z(n):
        return remote(mine.at[(zl + n + 1) % NZ], zbuf.at[n], pz_s.at[n], pz_r.at[n], zs_all[n])

    def taps_z(n):
        return remote(tmine, tzbuf.at[n], pt_s.at[n], pt_r.at[n], zs_all[n])

    def back_z(n):
        return remote(other.at[y, zl], other.at[y, zl], bz_s.at[n], bz_r.at[n], zs_all[n])

    def back_y(n):
        return remote(other.at[y], other.at[y], by_s.at[n], by_r.at[n], ys[n])

    for n in range(3):
        to_y(n).start()

    @pl.when(ctx < last_ctx)
    def _():
        head_copy.wait_recv()

    @pl.loop(0, 4)
    def _(l):
        lanes = lane(l)
        glb[T:, lanes] = head_in[:128, lanes].astype(F32)
        full = glb[:, lanes]
        rg[0] = full
        for r in range(1, 8):
            rg[r] = pltpu.roll(full, full.shape[0] - r, 0)
        pair_grad = convolve(lambda r, at: rg[r, pl.ds(at, T)], 0, 1, lanes)
        key_grad = pair_grad * vf[:, lanes]
        value_grad = pair_grad * kf[:, lanes]
        gk[:, lanes] = key_grad
        gv[:, lanes] = value_grad
        lead[0, :, lanes] = key_grad[:TAIL].astype(BF16)
        lead[1, :, lanes] = value_grad[:TAIL].astype(BF16)
        for b, (at, grad) in enumerate(
            ((0, gq[:, lanes]), (PRE, key_grad), (2 * PRE, value_grad))
        ):
            raw = jnp.concatenate(
                [halo[at : at + TAIL, lanes].astype(F32), br_ref[b, :, lanes].astype(F32)], axis=0
            )
            for i in range(3):
                moved = raw if i == 0 else pltpu.roll(raw, i, 0)
                tg[3 * b + i : 3 * b + i + 1, lanes] = jnp.sum(grad * moved[TAIL:], axis=0, keepdims=True)
        tpart[l] = tg[:, lanes].astype(BF16)

    lead_copy = remote(lead, lead_in, h_s.at[4], h_r.at[4], prv)

    @pl.when(ctx > 0)
    def _():
        lead_copy.start()

    for n in range(3):
        taps_y(n).start()

    value = part[y].astype(F32)
    for n in range(3):
        to_y(n).wait_recv()
        value = value + ybuf[n].astype(F32)
    mine[...] = value.astype(BF16)
    for n in range(NZ - 1):
        to_z(n).start()

    @pl.when(ctx < last_ctx)
    def _():
        lead_copy.wait_recv()

    @pl.loop(0, 4)
    def _(l):
        lanes = lane(l)
        for b, (grad, ahead) in enumerate(
            ((gq, head_in[128:, lanes]), (gk, lead_in[0, :, lanes]), (gv, lead_in[1, :, lanes]))
        ):
            full = jnp.concatenate([grad[:, lanes], ahead.astype(F32)], axis=0)
            value = taps_ref[3 * b : 3 * b + 1, lanes] * full
            for i in (1, 2):
                value = value + taps_ref[3 * b + i : 3 * b + i + 1, lanes] * pltpu.roll(full, T + TAIL - i, 0)
            gin_ref[b, :, lanes] = value[:T].astype(BF16)

    value = tpart[y].astype(F32)
    for n in range(3):
        taps_y(n).wait_recv()
        value = value + tybuf[n].astype(F32)
    tmine[...] = value.astype(BF16)
    for n in range(NZ - 1):
        taps_z(n).start()
    value = mine[zl].astype(F32)
    for n in range(NZ - 1):
        to_z(n).wait_recv()
        value = value + zbuf[n].astype(F32)
    other[y, zl] = value.astype(BF16)
    for n in range(NZ - 1):
        back_z(n).start()

    out_far.wait()
    for k in (0, 1):
        near[k] = (sums[zh, k].astype(F32) + far[k].astype(F32)).astype(BF16)
    m_sib = remote(near.at[1 - c], come.at[c], sib_s.at[4], sib_r.at[4], sib)
    m_sib.start()

    value = tmine[...].astype(F32)
    for n in range(NZ - 1):
        taps_z(n).wait_recv()
        value = value + tzbuf[n].astype(F32)
    other[y, NZ] = value.astype(BF16)
    for n in range(NZ - 1):
        back_z(n).wait()
    for n in range(3):
        back_y(n).start()
    m_sib.wait()
    for k in (0, 1):
        for zs in range(NZ):
            for yy in range(NY):
                at = (zs * NY + yy) * 256
                lanes = slice(yy * 128, (yy + 1) * 128)

                @pl.when(c == k)
                def _(zs=zs, lanes=lanes, at=at, k=k):
                    mixed_ref[:, at + k * 128 : at + (k + 1) * 128] = near[k, zs, :, lanes][:12]

                @pl.when(c != k)
                def _(zs=zs, lanes=lanes, at=at, k=k):
                    mixed_ref[:, at + k * 128 : at + (k + 1) * 128] = come[k, zs, :, lanes][:12]

    for n in range(3):
        back_y(n).wait()
    for l in range(4):
        for t in range(8):
            gfil_ref[t, :, l * 128 : (l + 1) * 128] = other[l, t].astype(F32)
        gtap_ref[:, l * 128 : (l + 1) * 128] = other[l, NZ].astype(F32)
    for n in range(3):
        to_y(n).wait_send()
        taps_y(n).wait_send()
    for n in range(NZ - 1):
        to_z(n).wait_send()
        taps_z(n).wait_send()

    @pl.when(ctx > 0)
    def _():
        head_copy.wait_send()
        lead_copy.wait_send()

    @pl.when(ctx < last_ctx)
    def _():
        for copy in halo_copies:
            copy.wait_send()

    @pl.loop(0, NZ)
    def _(zs):
        for h in (0, 1):
            y_plus(zs, y, h, 0).wait_send()
            y_minus(zs, y, h, 1).wait_send()
            y_plus(zs, y, h, 2).wait_send()

            @pl.when((zs <= zl) & (zl < NZ - 1))
            def _():
                z_right(zs, h).wait_send()

            @pl.when((zs >= zl) & (zl > 0))
            def _():
                z_left(zs, h).wait_send()

        for n in range(3):
            out_x(zs, n).wait_send()

    for k in (0, 1):
        cot_z(k).wait_send()
        for half in (0, 1):
            for n in range(3):
                cot_x(half, k, n).wait_send()


def block(branches, taps, filt, weight, cot):
    rows = weight.shape[0]
    wide = branches.shape[2]
    dma = pltpu.SemaphoreType.DMA
    vmem = pl.BlockSpec(memory_space=pltpu.VMEM)

    def f32(*shape):
        return pltpu.VMEM(shape, F32)

    def b16(*shape):
        return pltpu.VMEM(shape, BF16)

    return pl.pallas_call(
        block_kernel,
        out_shape=(
            jax.ShapeDtypeStruct((12, 8192), BF16),
            jax.ShapeDtypeStruct(branches.shape, BF16),
            jax.ShapeDtypeStruct(filt.shape, F32),
            jax.ShapeDtypeStruct((16, wide), F32),
        ),
        in_specs=[vmem] * 5,
        out_specs=(vmem,) * 4,
        scratch_shapes=[
            b16(NZ * NY, 2 * rows, 128), b16(4 * NX, 96, 512), b16(NZ, 256, 512), b16(TAIL + 2 * PRE, wide),
            f32(T, wide), f32(T, wide), f32(T, wide), f32(T, wide), f32(8, T + PRE, wide),
            b16(256, wide), b16(2, 256, wide), f32(2, 256, wide),
            b16(NZ, NX, 2, 32, 512), b16(NZ, 3, 2, 32, 512), b16(256, wide), b16(256, wide),
            b16(2, 2, NZ, 16, 512), b16(2, NZ, 16, 512), b16(2, NZ, 16, 512), b16(2, NZ, 16, 512),
            b16(NY, NZ + 1, 16, 128),
            f32(T + 128, wide), f32(8, T + 128, 128), f32(T, wide), f32(T, wide), f32(T, wide),
            b16(128 + TAIL, wide), b16(128 + TAIL, wide), b16(2, TAIL, wide), b16(2, TAIL, wide), f32(16, wide),
            b16(NY, NZ, 16, 128), b16(NZ, 16, 128), b16(3, NZ, 16, 128), b16(NZ - 1, 16, 128), f32(8, 16, wide),
            b16(NY, 16, 128), b16(16, 128), b16(3, 16, 128), b16(NZ - 1, 16, 128),
            dma((3,)), dma((5,)), dma((5,)),
            dma((2, NZ, 2)), dma((NZ, 2)), dma((3, NZ, 2)), dma((3, NZ, 2)),
            dma((2, 2, 3)), dma((2, 2, 3)), dma((NZ, 3)), dma((NZ, 3)), dma((3,)), dma((3,)), dma((5,)), dma((5,)),
            dma((3,)), dma((3,)), dma((NZ - 1,)), dma((NZ - 1,)), dma((NZ - 1,)), dma((NZ - 1,)),
            dma((NZ - 1,)), dma((NZ - 1,)), dma((3,)), dma((3,)), dma((3,)), dma((3,)),
        ],
        compiler_params=pltpu.CompilerParams(
            collective_id=0, has_side_effects=True, vmem_limit_bytes=56 * 2**20
        ),
        name="hyena_block",
    )(branches, taps, filt, weight, cot)


def body(branch_inputs, feat_taps, long_filter, out_weight, cotangent):
    own_rows = cotangent.shape[0]
    chan_count = branch_inputs.shape[2]
    tap_count = feat_taps.shape[1]
    cot_halves = (
        cotangent.reshape(own_rows, NZ, NY, 2, 128).transpose(3, 1, 0, 2, 4).reshape(2, NZ * own_rows, 512)
    )
    taps = feat_taps.astype(F32).reshape(3 * tap_count, chan_count)
    filt = long_filter.reshape(16, 8, chan_count).transpose(1, 0, 2)
    mixed_out, grad_inputs, grad_filter, grad_taps = block(branch_inputs, taps, filt, out_weight, cot_halves)
    grad_filter = grad_filter.transpose(1, 0, 2).reshape(long_filter.shape)
    return mixed_out, grad_inputs, grad_filter, grad_taps[:9].reshape(3, tap_count, chan_count)


def solution(mesh):
    placed = (
        P(None, "ctx", "tp"),
        P(None, None, "tp"),
        P(None, "tp"),
        P("tp", "ctx"),
        P(("ctx", "tp"), None),
    )
    return jax.shard_map(
        body,
        mesh=mesh,
        in_specs=placed,
        out_specs=(
            P(("ctx", "tp"), None),
            P(None, "ctx", "tp"),
            P(None, "tp"),
            P(None, None, "tp"),
        ),
        check_vma=False,
    )
```

time: 227 us -> 173 us (0.76)
  starting transfers between devices: 29.9 us -> 0 us
  Pallas kernels: 133 us -> 160 us
  matrix products: 26.4 us -> 0 us
  local copies, waits for them, and re-layouts: 28.4 us -> 10 us
  other arithmetic: 6.85 us -> 0 us
    ppermute x4 -> x0, starting transfers between devices: 29.9 us -> none  [the longest x2 24.8 us: from_far(): lax.ppermute(value, 'tp', [(k, k ^ count // 2) for k in range(count)])]
    pallas_call x2 -> x1, Pallas kernels: 133 us -> 160 us  [block(): pl.pallas_call(block_kernel, out_shape=(jax.ShapeDtypeStruct((12, 8192),...]
    conv_general_dilated x8 -> x0, matrix products: 26.4 us -> none  [depthwise(): lax.conv_general_dilated(signal[None], kernel[:, None, :], (1,), 'VALID',...]
    reshape x17 -> x3, local copies, waits for them, and re-layouts: 12.9 us -> 3.63 us  [the longest x1 1.44 us: body(): grad_taps[:9].reshape(3, tap_count, chan_count)]
    convert_element_type x3 -> x0, other arithmetic: 2.8 us -> none  [the longest x1 1.74 us: body(): (out_near.astype(jnp.float32) + out_far.astype(jnp.float32)).astype(jnp.b...]
    squeeze x4 -> x0, local copies, waits for them, and re-layouts: 2.54 us -> none  [the longest x1 1.04 us: body(): branch_inputs[1, tok_count - reach_len:]]
  transfers between devices with their start and end apart: 4 -> 0, of which waited for: 0 -> 0; matrix products, arithmetic and copies ran while one was open for 20% -> 0% of each run, Pallas kernels for 0% -> 0%
where the time goes in v3:
time: 173 us; the launch traced here: 171 us
  Pallas kernels  160 us (92%)
  local copies, waits for them, and re-layouts  10 us (6%)
    pallas_call x1, Pallas kernels, block(): pl.pallas_call(block_kernel, out_shape=(jax.ShapeDtypeStruct((12, 8192),...  160 us

profile of v3, /device:TPU:6, one launch (start us, length us, event | category | flops | bytes accessed | tf_op | source)
XLA Modules:
  0.0 171.0 jit_solution(8731944376767527806)
XLA Ops:
  0.6 1.3 reshape.36.taps_ref
  2.0 1.1 reshape.31
  3.1 0.1 copy.18
  3.1 0.0 copy-start.1
  3.1 0.8 reshape.32.cot_ref
  3.9 0.2 copy-done.1
  4.1 0.9 copy.17
  4.9 160.3 %hyena_block.1 = (bf16[12,8192]{1,0:T(8,128)(2,1)}, bf16[3,192,512]{2,1,0:T(8,128)(2,1)}, f32[8,16,512]{2,1,0:T(8,128)}, f32[16,512]{1,0:T(8,128)}) custom-call(bf16[3,192,512]{2,1,0:T(8,128)(2,1)} %br_ref.1, f32[9,512]{1,0:T(8,128)} %reshape.36.taps_ref, f32[8,16,512]{2,1,0:T(8,128)} %bitcast.12, bf16[512,256]{1,0:T(8,128)(2,1)} %w_ref.1, ...), custom_call_target="tpu_custom_call" | custom-call | tf_op jit(solution)/shard_map/hyena_block/pallas_call | solution.py:589
  165.3 0.0 copy-start
  165.3 1.4 reshape.34
  166.7 1.8 %copy.16 = f32[16,8,512]{2,1,0:T(8,128)} copy(f32[16,8,512]{2,0,1:T(8,128)} %bitcast.16) | data formatting | bytes 524288 | tf_op jit(solution)/shard_map/transpose | solution.py:633
  168.5 1.7 copy.21
  170.2 0.0 copy-done
  170.2 0.8 copy.22
Async XLA Ops:
  3.1 1.0 copy-start.1
  165.3 4.9 %copy-start = (bf16[3,192,512]{2,1,0:T(8,128)(2,1)S(1)}, bf16[3,192,512]{2,1,0:T(8,128)(2,1)}, u32[]{:S(2)}) copy-start(bf16[3,192,512]{2,1,0:T(8,128)(2,1)} %get-tuple-element.17) | copy-start | bytes 1769476

commit v4 on v3

--- a/solution.py
+++ b/solution.py
@@ -50,12 +50,12 @@
 
 
 def block_kernel(
-    br_ref, taps_ref, fil_ref, w_ref, cot_ref,
+    br_ref, ftaps_ref, filt_ref, w_ref, cot_ref,
     mixed_ref, gin_ref, gfil_ref, gtap_ref,
-    wg, cp, cg, halo, qf, kf, vf, ls, rot, gated, both, acc, out, arrived, gsend, grecv,
+    taps_ref, fil_ref, wg, cp, cg, halo, qf, kf, vf, ls, rot, gated, both, acc, out, arrived, gsend, grecv,
     sums, far, near, come, other, glb, rg, gq, gk, gv, head, head_in, lead, lead_in, tg,
     part, mine, ybuf, zbuf, total, tpart, tmine, tybuf, tzbuf,
-    own_sem, sib_s, sib_r, z_s, z_r, y_s, y_r, x_s, x_r, o_s, o_r, zp_s, zp_r, h_s, h_r,
+    own_sem, sib_s, sib_r, z_s, z_r, y_s, y_r, x_s, x_r, o_s, o_r, zp_s, zp_r, f_s, f_r, h_s, h_r,
     py_s, py_r, pz_s, pz_r, pt_s, pt_r, bz_s, bz_r, by_s, by_r, ty_s, ty_r,
 ):
     ctx, tp, zl, y, zh, x, c = coords()
@@ -162,6 +162,10 @@
         cot_z(h).start()
         for n in range(3):
             cot_x(zh, h, n).start()
+    for b in range(3):
+        taps_ref[b] = ftaps_ref[b].astype(F32)
+    for j in range(128):
+        fil_ref[j % 8, j // 8 : j // 8 + 1] = filt_ref[j : j + 1]
     acc[...] = jnp.zeros_like(acc)
     tg[...] = jnp.zeros_like(tg)
 
@@ -197,9 +201,9 @@
 
         def feature(b, at, n):
             raw = jnp.concatenate([halo[at : at + n, lanes].astype(F32), br_ref[b, :, lanes].astype(F32)], axis=0)
-            value = taps_ref[3 * b : 3 * b + 1, lanes] * raw
+            value = taps_ref[b, 0:1, lanes] * raw
             for i in (1, 2):
-                value = value + taps_ref[3 * b + i : 3 * b + i + 1, lanes] * pltpu.roll(raw, i, 0)
+                value = value + taps_ref[b, i : i + 1, lanes] * pltpu.roll(raw, i, 0)
             return value.astype(BF16).astype(F32)
 
         query = feature(0, 0, TAIL)[TAIL:]
@@ -245,16 +249,19 @@
         value = value.astype(BF16)
         for half in (0, 1):
             for k in (0, 1):
-                sums[half, k, zs] = value[half, k * 16 : (k + 1) * 16]
-
-    def both_sides(step, act):
-        @pl.loop(0, 2)
-        def _(side):
-            zs = zl + (2 * side - 1) * step
-
-            @pl.when((step >= 0) & (zs >= 0) & (zs < NZ) & ((step > 0) | (side == 0)))
-            def _():
-                act(zs)
+                sums[half, zs, k] = value[half, k * 16 : (k + 1) * 16]
+
+    near_end = jnp.minimum(zl, NZ - 1 - zl)
+
+    def nth(n):
+        paired = jnp.where(n % 2 == 1, zl - (n + 1) // 2, zl + n // 2)
+        single = jnp.where(zl < NZ // 2, zl + (n - near_end), zl - (n - near_end))
+        return jnp.where(n <= 2 * near_end, paired, single)
+
+    def each(first, last, act):
+        @pl.loop(first, last)
+        def _(n):
+            act(nth(n))
 
     x_sib = remote(gated, both.at[c], sib_s.at[2], sib_r.at[2], sib)
     x_own = pltpu.make_async_copy(gated, both.at[c], own_sem.at[2])
@@ -296,8 +303,13 @@
             for h in (0, 1):
                 y_plus(zs, (y + 2) % NY, h, 2).wait_recv()
 
-        both_sides(step - 1, pass_on)
-        both_sides(step - 2, relayed)
+        @pl.when(step <= NZ)
+        def _():
+            pass_on(nth(step - 1))
+
+        @pl.when(step >= 2)
+        def _():
+            relayed(nth(step - 2))
 
         @pl.when((step == 1) & (ctx > 0))
         def _():
@@ -335,24 +347,19 @@
                 for zs, rows16 in enumerate(spaced(cp[piece].astype(F32), NZ)):
                     cg[zs, at] = rows16
 
-        @pl.loop(forward_done(step - 1), forward_done(step))
-        def _(when):
-            both_sides(when, forward)
-
-        @pl.loop(backward_done(step - 1), backward_done(step))
-        def _(when):
-            both_sides(when, backward)
-
-        @pl.loop(forward_done(step - 2), forward_done(step - 1))
-        def _(when):
-            both_sides(when, collect)
+        each(forward_done(step - 1), forward_done(step), forward)
+        each(backward_done(step - 1), backward_done(step), backward)
+        each(forward_done(step - 3), forward_done(step - 2), collect)
 
     gsend[...] = acc[1 - c].astype(BF16)
     g_sib = remote(gsend, grecv, sib_s.at[3], sib_r.at[3], sib)
     g_sib.start()
-    both_sides(jnp.int32(NZ - 1), collect)
-    out_far = remote(sums.at[1 - zh], far, zp_s.at[2], zp_r.at[2], zpart)
-    out_far.start()
+
+    def out_far(zs):
+        return remote(sums.at[1 - zh, zs], far.at[zs], f_s.at[zs], f_r.at[zs], zpart)
+
+    done = forward_done(NZ - 1)
+    each(0, done, lambda zs: out_far(zs).start())
     g_sib.wait()
 
     def gradients(l):
@@ -417,6 +424,12 @@
 
     for n in range(3):
         to_y(n).start()
+
+    def finish(zs):
+        collect(zs)
+        out_far(zs).start()
+
+    each(done, NZ, finish)
 
     @pl.when(ctx < last_ctx)
     def _():
@@ -476,9 +489,9 @@
             ((gq, head_in[128:, lanes]), (gk, lead_in[0, :, lanes]), (gv, lead_in[1, :, lanes]))
         ):
             full = jnp.concatenate([grad[:, lanes], ahead.astype(F32)], axis=0)
-            value = taps_ref[3 * b : 3 * b + 1, lanes] * full
+            value = taps_ref[b, 0:1, lanes] * full
             for i in (1, 2):
-                value = value + taps_ref[3 * b + i : 3 * b + i + 1, lanes] * pltpu.roll(full, T + TAIL - i, 0)
+                value = value + taps_ref[b, i : i + 1, lanes] * pltpu.roll(full, T + TAIL - i, 0)
             gin_ref[b, :, lanes] = value[:T].astype(BF16)
 
     value = tpart[y].astype(F32)
@@ -496,9 +509,10 @@
     for n in range(NZ - 1):
         back_z(n).start()
 
-    out_far.wait()
-    for k in (0, 1):
-        near[k] = (sums[zh, k].astype(F32) + far[k].astype(F32)).astype(BF16)
+    for zs in range(NZ):
+        out_far(zs).wait()
+        for k in (0, 1):
+            near[k, zs] = (sums[zh, zs, k].astype(F32) + far[zs, k].astype(F32)).astype(BF16)
     m_sib = remote(near.at[1 - c], come.at[c], sib_s.at[4], sib_r.at[4], sib)
     m_sib.start()
 
@@ -530,8 +544,12 @@
         back_y(n).wait()
     for l in range(4):
         for t in range(8):
-            gfil_ref[t, :, l * 128 : (l + 1) * 128] = other[l, t].astype(F32)
-        gtap_ref[:, l * 128 : (l + 1) * 128] = other[l, NZ].astype(F32)
+            total[t, :, l * 128 : (l + 1) * 128] = other[l, t].astype(F32)
+        tg[:, l * 128 : (l + 1) * 128] = other[l, NZ].astype(F32)
+    for j in range(128):
+        gfil_ref[j : j + 1] = total[j % 8, j // 8 : j // 8 + 1]
+    for b in range(3):
+        gtap_ref[b] = tg[3 * b : 3 * b + 3]
     for n in range(3):
         to_y(n).wait_send()
         taps_y(n).wait_send()
@@ -592,16 +610,17 @@
             jax.ShapeDtypeStruct((12, 8192), BF16),
             jax.ShapeDtypeStruct(branches.shape, BF16),
             jax.ShapeDtypeStruct(filt.shape, F32),
-            jax.ShapeDtypeStruct((16, wide), F32),
+            jax.ShapeDtypeStruct(taps.shape, F32),
         ),
         in_specs=[vmem] * 5,
         out_specs=(vmem,) * 4,
         scratch_shapes=[
+            f32(*taps.shape), f32(8, 16, wide),
             b16(NZ * NY, 2 * rows, 128), b16(4 * NX, 96, 512), b16(NZ, 256, 512), b16(TAIL + 2 * PRE, wide),
             f32(T, wide), f32(T, wide), f32(T, wide), f32(T, wide), f32(8, T + PRE, wide),
             b16(256, wide), b16(2, 256, wide), f32(2, 256, wide),
             b16(NZ, NX, 2, 32, 512), b16(NZ, 3, 2, 32, 512), b16(256, wide), b16(256, wide),
-            b16(2, 2, NZ, 16, 512), b16(2, NZ, 16, 512), b16(2, NZ, 16, 512), b16(2, NZ, 16, 512),
+            b16(2, NZ, 2, 16, 512), b16(NZ, 2, 16, 512), b16(2, NZ, 16, 512), b16(2, NZ, 16, 512),
             b16(NY, NZ + 1, 16, 128),
             f32(T + 128, wide), f32(8, T + 128, 128), f32(T, wide), f32(T, wide), f32(T, wide),
             b16(128 + TAIL, wide), b16(128 + TAIL, wide), b16(2, TAIL, wide), b16(2, TAIL, wide), f32(16, wide),
@@ -609,7 +628,7 @@
             b16(NY, 16, 128), b16(16, 128), b16(3, 16, 128), b16(NZ - 1, 16, 128),
             dma((3,)), dma((5,)), dma((5,)),
             dma((2, NZ, 2)), dma((NZ, 2)), dma((3, NZ, 2)), dma((3, NZ, 2)),
-            dma((2, 2, 3)), dma((2, 2, 3)), dma((NZ, 3)), dma((NZ, 3)), dma((3,)), dma((3,)), dma((5,)), dma((5,)),
+            dma((2, 2, 3)), dma((2, 2, 3)), dma((NZ, 3)), dma((NZ, 3)), dma((2,)), dma((2,)), dma((NZ,)), dma((NZ,)), dma((5,)), dma((5,)),
             dma((3,)), dma((3,)), dma((NZ - 1,)), dma((NZ - 1,)), dma((NZ - 1,)), dma((NZ - 1,)),
             dma((NZ - 1,)), dma((NZ - 1,)), dma((3,)), dma((3,)), dma((3,)), dma((3,)),
         ],
@@ -622,16 +641,10 @@
 
 def body(branch_inputs, feat_taps, long_filter, out_weight, cotangent):
     own_rows = cotangent.shape[0]
-    chan_count = branch_inputs.shape[2]
-    tap_count = feat_taps.shape[1]
     cot_halves = (
         cotangent.reshape(own_rows, NZ, NY, 2, 128).transpose(3, 1, 0, 2, 4).reshape(2, NZ * own_rows, 512)
     )
-    taps = feat_taps.astype(F32).reshape(3 * tap_count, chan_count)
-    filt = long_filter.reshape(16, 8, chan_count).transpose(1, 0, 2)
-    mixed_out, grad_inputs, grad_filter, grad_taps = block(branch_inputs, taps, filt, out_weight, cot_halves)
-    grad_filter = grad_filter.transpose(1, 0, 2).reshape(long_filter.shape)
-    return mixed_out, grad_inputs, grad_filter, grad_taps[:9].reshape(3, tap_count, chan_count)
+    return block(branch_inputs, feat_taps, long_filter, out_weight, cot_halves)
 
 
 def solution(mesh):

time: 173 us -> 163 us (0.942)
  Pallas kernels: 160 us -> 155 us
  local copies, waits for them, and re-layouts: 10 us -> 6.88 us
    pallas_call x1, Pallas kernels: 160 us -> 155 us  [block(): pl.pallas_call(block_kernel, out_shape=(jax.ShapeDtypeStruct((12, 8192),...]
    reshape x3 -> x0, local copies, waits for them, and re-layouts: 3.63 us -> none  [the longest x1 1.44 us: body(): grad_taps[:9].reshape(3, tap_count, chan_count)]
    unnamed x6 -> x8, local copies, waits for them, and re-layouts: 2.68 us -> 4.98 us
    transpose x1 -> x0, local copies, waits for them, and re-layouts: 1.81 us -> none  [body(): grad_filter = grad_filter.transpose(1, 0, 2).reshape(long_filter.shape)]
where the time goes in v4:
time: 163 us; the launch traced here: 162 us
  Pallas kernels  155 us (95%)
  local copies, waits for them, and re-layouts  6.88 us (4%)
    pallas_call x1, Pallas kernels, block(): pl.pallas_call(block_kernel, out_shape=(jax.ShapeDtypeStruct((12, 8192),...  155 us
    unnamed x8, local copies, waits for them, and re-layouts  4.98 us

profile of v4, /device:TPU:6, one launch (start us, length us, event | category | flops | bytes accessed | tf_op | source)
XLA Modules:
  0.0 162.4 jit_solution(6125007593366032597)
XLA Ops:
  0.6 1.1 reshape.14
  1.7 0.1 copy.11
  1.8 0.8 reshape.15.cot_ref
  2.5 154.9 %hyena_block.1 = (bf16[12,8192]{1,0:T(8,128)(2,1)}, bf16[3,192,512]{2,1,0:T(8,128)(2,1)}, f32[128,512]{1,0:T(8,128)}, f32[3,3,512]{2,1,0:T(4,128)}) custom-call(bf16[3,192,512]{2,1,0:T(8,128)(2,1)} %br_ref.1, bf16[3,3,512]{2,1,0:T(4,128)(2,1)} %ftaps_ref.1, f32[128,512]{1,0:T(8,128)} %filt_ref.1, bf16[512,256]{1,0:T(8,128)(2,1)} %w_ref.1, ...), custom_call_target="tpu_custom_call" | custom-call | tf_op jit(solution)/shard_map/hyena_block/pallas_call | solution.py:607
  157.4 1.7 %copy.16 = bf16[12,8192]{1,0:T(8,128)(2,1)} copy(bf16[12,8192]{1,0:T(8,128)(2,1)} %get-tuple-element.8) | data formatting | bytes 393216
  159.1 0.0 copy-start
  159.1 2.0 %copy.17 = bf16[3,192,512]{2,1,0:T(8,128)(2,1)} copy(bf16[3,192,512]{2,1,0:T(8,128)(2,1)} %get-tuple-element.9) | data formatting | bytes 1179648
  161.1 0.0 copy-done
  161.1 0.0 copy-start.1
  161.1 0.7 copy.18
  161.8 0.0 copy-done.1
  161.8 0.6 copy.19
Async XLA Ops:
  159.1 2.0 %copy-start = (f32[128,512]{1,0:T(8,128)S(1)}, f32[128,512]{1,0:T(8,128)}, u32[]{:S(2)}) copy-start(f32[128,512]{1,0:T(8,128)} %get-tuple-element.10) | copy-start | bytes 786436
  161.1 0.7 copy-start.1

commit v5 on v4

--- a/solution.py
+++ b/solution.py
@@ -121,11 +121,13 @@
         y_plus(zs, (y + 3) % NY, h, 0).wait_recv()
         y_minus(zs, (y + 1) % NY, h, 1).wait_recv()
 
-        @pl.when(h == 0)
+        upward = (h == 0) & (zs != zl)
+
+        @pl.when(upward)
         def _():
             y_plus(zs, (y + 3) % NY, h, 2).start()
 
-        @pl.when(h == 1)
+        @pl.when(jnp.logical_not(upward))
         def _():
             y_minus(zs, (y + 1) % NY, h, 2).start()
 
@@ -187,6 +189,11 @@
             at = 12 * i
             yield (value[at : at + 16] if at % 8 == 0 else shifted[at - 4 : at + 12]).astype(BF16)
 
+    def dense(value):
+        low = lax.broadcasted_iota(jnp.int32, (8, value.shape[1]), 0) < 4
+        up, down = pltpu.roll(value[16:24], 4, 0), pltpu.roll(value[24:32], 4, 0)
+        return [value[:8], jnp.where(low, value[8:16], up), jnp.where(low, up, down)]
+
     def convolve(source, first, step, lanes):
         def residue(r, value):
             for q in range(16):
@@ -227,11 +234,12 @@
     def forward(zs):
         value = jnp.dot(both[0], weight(zs, 0), preferred_element_type=F32)
         value = value + jnp.dot(both[1], weight(zs, 1), preferred_element_type=F32)
-        value = value.astype(BF16)
-        for half in (0, 1):
-            for xx in range(NX):
+        for xx in range(NX):
+            groups = []
+            for half in (0, 1):
                 at = (half * NX + xx) * 32
-                out[zs, xx, half] = value[at : at + 32]
+                groups += dense(value[at : at + 32])
+            out[zs, xx] = jnp.concatenate(groups, axis=0).astype(BF16)
         for n in range(3):
             out_x(zs, n).start()
 
@@ -246,10 +254,12 @@
         for n in range(3):
             out_x(zs, n).wait_recv()
             value = value + arrived[zs, n].astype(F32)
-        value = value.astype(BF16)
         for half in (0, 1):
-            for k in (0, 1):
-                sums[half, zs, k] = value[half, k * 16 : (k + 1) * 16]
+            own = value[24 * half : 24 * half + 24]
+            sums[half, zs] = jnp.concatenate([own[:, :256], own[:, 256:]], axis=0).astype(BF16)
+
+    def out_far(zs):
+        return remote(sums.at[1 - zh, zs], far.at[zs], f_s.at[zs], f_r.at[zs], zpart)
 
     near_end = jnp.minimum(zl, NZ - 1 - zl)
 
@@ -267,7 +277,7 @@
     x_own = pltpu.make_async_copy(gated, both.at[c], own_sem.at[2])
 
     def forward_done(step):
-        return jnp.maximum(0, jnp.minimum(2 * (step - 4), step - 1))
+        return jnp.maximum(0, jnp.minimum(2 * (step - 2), step - 1))
 
     def backward_done(step):
         return jnp.maximum(0, jnp.minimum(3 * (step - 5), step - 1))
@@ -283,8 +293,6 @@
                 def _():
                     z_right(zl - step, h).start()
 
-                spread(zl - step, h)
-
             @pl.when(zl + step < NZ)
             def _(h=h):
                 z_left(zl + step, h).wait_recv()
@@ -293,8 +301,6 @@
                 def _():
                     z_left(zl + step, h).start()
 
-                spread(zl + step, h)
-
         def pass_on(zs):
             for h in order:
                 relay(zs, h)
@@ -303,6 +309,11 @@
             for h in (0, 1):
                 y_plus(zs, (y + 2) % NY, h, 2).wait_recv()
 
+        @pl.when(step < NZ)
+        def _():
+            for h in order:
+                spread(nth(step), h)
+
         @pl.when(step <= NZ)
         def _():
             pass_on(nth(step - 1))
@@ -316,20 +327,25 @@
             for copy in halo_copies:
                 copy.wait_recv()
 
-        @pl.when(step <= 4)
-        def _():
-            features(step - 1)
-
-        @pl.when(step == 4)
+        @pl.when(step <= 2)
+        def _():
+            @pl.loop(2 * step - 2, 2 * step)
+            def _(l):
+                features(l)
+
+        @pl.when(step == 2)
         def _():
             x_sib.start()
             x_own.start()
+
+        @pl.when(step == 4)
+        def _():
             for k in order:
                 cot_z(k).wait_recv()
                 for n in range(3):
                     cot_x(1 - zh, k, n).start()
 
-        @pl.when(step == 5)
+        @pl.when(step == 3)
         def _():
             x_own.wait()
             x_sib.wait()
@@ -351,26 +367,23 @@
         each(backward_done(step - 1), backward_done(step), backward)
         each(forward_done(step - 3), forward_done(step - 2), collect)
 
+        @pl.when(step >= NZ - 1)
+        def _():
+            each(jnp.where(step == NZ - 1, 0, forward_done(step - 3)), forward_done(step - 2), lambda zs: out_far(zs).start())
+
     gsend[...] = acc[1 - c].astype(BF16)
     g_sib = remote(gsend, grecv, sib_s.at[3], sib_r.at[3], sib)
     g_sib.start()
 
-    def out_far(zs):
-        return remote(sums.at[1 - zh, zs], far.at[zs], f_s.at[zs], f_r.at[zs], zpart)
-
-    done = forward_done(NZ - 1)
-    each(0, done, lambda zs: out_far(zs).start())
     g_sib.wait()
 
     def gradients(l):
         lanes = lane(l)
-        low = lax.broadcasted_iota(jnp.int32, (8, 128), 0) < 4
         tiles = []
         for m in range(8):
             at = 32 * m
             block = acc[c, at : at + 32, lanes] + grecv[at : at + 32, lanes].astype(F32)
-            up, down = pltpu.roll(block[16:24], 4, 0), pltpu.roll(block[24:32], 4, 0)
-            tiles += [block[:8], jnp.where(low, block[8:16], up), jnp.where(low, up, down)]
+            tiles += dense(block)
         mixed_grad = jnp.concatenate(tiles, axis=0)
         long_grad = mixed_grad * qf[:, lanes]
         query_grad = mixed_grad * ls[:, lanes]
@@ -429,7 +442,7 @@
         collect(zs)
         out_far(zs).start()
 
-    each(done, NZ, finish)
+    each(forward_done(NZ - 1), NZ, finish)
 
     @pl.when(ctx < last_ctx)
     def _():
@@ -478,6 +491,14 @@
     for n in range(NZ - 1):
         to_z(n).start()
 
+    value = tpart[y].astype(F32)
+    for n in range(3):
+        taps_y(n).wait_recv()
+        value = value + tybuf[n].astype(F32)
+    tmine[...] = value.astype(BF16)
+    for n in range(NZ - 1):
+        taps_z(n).start()
+
     @pl.when(ctx < last_ctx)
     def _():
         lead_copy.wait_recv()
@@ -494,13 +515,6 @@
                 value = value + taps_ref[b, i : i + 1, lanes] * pltpu.roll(full, T + TAIL - i, 0)
             gin_ref[b, :, lanes] = value[:T].astype(BF16)
 
-    value = tpart[y].astype(F32)
-    for n in range(3):
-        taps_y(n).wait_recv()
-        value = value + tybuf[n].astype(F32)
-    tmine[...] = value.astype(BF16)
-    for n in range(NZ - 1):
-        taps_z(n).start()
     value = mine[zl].astype(F32)
     for n in range(NZ - 1):
         to_z(n).wait_recv()
@@ -511,8 +525,10 @@
 
     for zs in range(NZ):
         out_far(zs).wait()
-        for k in (0, 1):
-            near[k, zs] = (sums[zh, zs, k].astype(F32) + far[zs, k].astype(F32)).astype(BF16)
+        value = sums[zh, zs].astype(F32) + far[zs].astype(F32)
+        value = jnp.concatenate([value[:24], value[24:]], axis=1)
+        for k, rows16 in enumerate(spaced(value, 2)):
+            near[k, zs] = rows16
     m_sib = remote(near.at[1 - c], come.at[c], sib_s.at[4], sib_r.at[4], sib)
     m_sib.start()
 
@@ -619,8 +635,8 @@
             b16(NZ * NY, 2 * rows, 128), b16(4 * NX, 96, 512), b16(NZ, 256, 512), b16(TAIL + 2 * PRE, wide),
             f32(T, wide), f32(T, wide), f32(T, wide), f32(T, wide), f32(8, T + PRE, wide),
             b16(256, wide), b16(2, 256, wide), f32(2, 256, wide),
-            b16(NZ, NX, 2, 32, 512), b16(NZ, 3, 2, 32, 512), b16(256, wide), b16(256, wide),
-            b16(2, NZ, 2, 16, 512), b16(NZ, 2, 16, 512), b16(2, NZ, 16, 512), b16(2, NZ, 16, 512),
+            b16(NZ, NX, 48, 512), b16(NZ, 3, 48, 512), b16(256, wide), b16(256, wide),
+            b16(2, NZ, 48, 256), b16(NZ, 48, 256), b16(2, NZ, 16, 512), b16(2, NZ, 16, 512),
             b16(NY, NZ + 1, 16, 128),
             f32(T + 128, wide), f32(8, T + 128, 128), f32(T, wide), f32(T, wide), f32(T, wide),
             b16(128 + TAIL, wide), b16(128 + TAIL, wide), b16(2, TAIL, wide), b16(2, TAIL, wide), f32(16, wide),

time: 163 us -> 154 us (0.945)
  Pallas kernels: 155 us -> 147 us
    pallas_call x1, Pallas kernels: 155 us -> 147 us  [block(): pl.pallas_call(block_kernel, out_shape=(jax.ShapeDtypeStruct((12, 8192),...]
where the time goes in v5:
time: 154 us
  Pallas kernels  147 us (95%)
  local copies, waits for them, and re-layouts  6.88 us (4%)
    pallas_call x1, Pallas kernels, block(): pl.pallas_call(block_kernel, out_shape=(jax.ShapeDtypeStruct((12, 8192),...  147 us
    unnamed x8, local copies, waits for them, and re-layouts  4.98 us

profile of v5, /device:TPU:6, one launch (start us, length us, event | category | flops | bytes accessed | tf_op | source)
XLA Modules:
  0.0 154.1 jit_solution(12719067039401087442)
XLA Ops:
  0.6 1.1 reshape.14
  1.7 0.1 copy.11
  1.8 0.8 reshape.15.cot_ref
  2.5 146.5 %hyena_block.1 = (bf16[12,8192]{1,0:T(8,128)(2,1)}, bf16[3,192,512]{2,1,0:T(8,128)(2,1)}, f32[128,512]{1,0:T(8,128)}, f32[3,3,512]{2,1,0:T(4,128)}) custom-call(bf16[3,192,512]{2,1,0:T(8,128)(2,1)} %br_ref.1, bf16[3,3,512]{2,1,0:T(4,128)(2,1)} %ftaps_ref.1, f32[128,512]{1,0:T(8,128)} %filt_ref.1, bf16[512,256]{1,0:T(8,128)(2,1)} %w_ref.1, ...), custom_call_target="tpu_custom_call" | custom-call | tf_op jit(solution)/shard_map/hyena_block/pallas_call | solution.py:623
  149.1 1.7 %copy.16 = bf16[12,8192]{1,0:T(8,128)(2,1)} copy(bf16[12,8192]{1,0:T(8,128)(2,1)} %get-tuple-element.8) | data formatting | bytes 393216
  150.7 0.0 copy-start
  150.7 2.0 %copy.17 = bf16[3,192,512]{2,1,0:T(8,128)(2,1)} copy(bf16[3,192,512]{2,1,0:T(8,128)(2,1)} %get-tuple-element.9) | data formatting | bytes 1179648
  152.7 0.0 copy-done
  152.7 0.0 copy-start.1
  152.7 0.7 copy.18
  153.4 0.0 copy-done.1
  153.4 0.6 copy.19
Async XLA Ops:
  150.7 2.0 %copy-start = (f32[128,512]{1,0:T(8,128)S(1)}, f32[128,512]{1,0:T(8,128)}, u32[]{:S(2)}) copy-start(f32[128,512]{1,0:T(8,128)} %get-tuple-element.10) | copy-start | bytes 786436
  152.7 0.7 copy-start.1

commit v6 on v5

--- a/solution.py
+++ b/solution.py
@@ -50,17 +50,19 @@
 
 
 def block_kernel(
-    br_ref, ftaps_ref, filt_ref, w_ref, cot_ref,
+    br_ref, ftaps_ref, filt_ref, w_ref, cot_in,
     mixed_ref, gin_ref, gfil_ref, gtap_ref,
-    taps_ref, fil_ref, wg, cp, cg, halo, qf, kf, vf, ls, rot, gated, both, acc, out, arrived, gsend, grecv,
+    cot16, cot_ref, taps_ref, fil_ref, wg, cp, cg, halo, qf, kf, vf, ls, rot, gated, both, acc, out, arrived, gsend, grecv,
     sums, far, near, come, other, glb, rg, gq, gk, gv, head, head_in, lead, lead_in, tg,
     part, mine, ybuf, zbuf, total, tpart, tmine, tybuf, tzbuf,
-    own_sem, sib_s, sib_r, z_s, z_r, y_s, y_r, x_s, x_r, o_s, o_r, zp_s, zp_r, f_s, f_r, h_s, h_r,
+    own_sem, sib_s, sib_r, cy_s, cy_r, xp_s, xp_r, g_s, g_r, m_s, m_r, z_s, z_r, y_s, y_r, x_s, x_r, o_s, o_r, zp_s, zp_r, f_s, f_r, h_s, h_r,
     py_s, py_r, pz_s, pz_r, pt_s, pt_r, bz_s, bz_r, by_s, by_r, ty_s, ty_r,
 ):
     ctx, tp, zl, y, zh, x, c = coords()
-    yp = device(zl, (y + 1) % NY, zh, x, c)
-    ym = device(zl, (y + 3) % NY, zh, x, c)
+    t = y % 2
+    yx, ps, js = y + 1 - 2 * t, ((y + 1) // 2) % 2, y // 2
+    wy = device(zl, 3 - y, zh, x, c)
+    part_same, part_other = device(zl, yx, zh, x, c), device(zl, yx, zh, x, 1 - c)
     sib = device(zl, y, zh, x, 1 - c)
     zpart = device(zl, y, 1 - zh, x, c)
     xs = [device(zl, y, zh, (x + k) % NX, c) for k in (1, 2, 3)]
@@ -72,25 +74,27 @@
     nxt = {"ctx": jnp.minimum(ctx + 1, last_ctx), "tp": tp}
     prv = {"ctx": jnp.maximum(ctx - 1, 0), "tp": tp}
     greet(
-        [(sib, True), (zpart, True)]
+        [(sib, True), (zpart, True), (part_other, True)]
         + [(d, True) for d in xs + ys + zs_all]
         + [(nxt, ctx < last_ctx), (prv, ctx > 0)]
     )
     rows = w_ref.shape[0]
 
-    def unit(zs, yy, h):
-        return wg.at[zs * NY + yy, pl.ds(pl.multiple_of(h * rows, rows), rows)]
+    def unit(zs, j, h):
+        return wg.at[zs * 2 + j, pl.ds(pl.multiple_of(h * rows, rows), rows)]
+
+    def token_rows(which):
+        return pl.ds(pl.multiple_of(which * 256, 256), 256)
+
+    def cot_rows(which):
+        return pl.ds(pl.multiple_of(which * 96, 96), 96)
 
     keep = w_ref.at[:, pl.ds(pl.multiple_of(c * 128, 128), 128)]
     give = w_ref.at[:, pl.ds(pl.multiple_of((1 - c) * 128, 128), 128)]
-    w_sib = remote(give, unit(zl, y, c), sib_s.at[0], sib_r.at[0], sib)
+    w_sib = remote(give, unit(zl, js, c), sib_s.at[0], sib_r.at[0], sib)
     w_sib.start()
-    w_own = pltpu.make_async_copy(keep, unit(zl, y, c), own_sem.at[0])
+    w_own = pltpu.make_async_copy(keep, unit(zl, js, c), own_sem.at[0])
     w_own.start()
-    c_sib = remote(cot_ref.at[1 - c], cp.at[tp], sib_s.at[1], sib_r.at[1], sib)
-    c_sib.start()
-    c_own = pltpu.make_async_copy(cot_ref.at[c], cp.at[tp], own_sem.at[1])
-    c_own.start()
     halo_copies = [
         remote(br_ref.at[b, pl.ds(T - n, n)], halo.at[pl.ds(at, n)], h_s.at[b], h_r.at[b], nxt)
         for b, n, at in ((0, TAIL, 0), (1, PRE, TAIL), (2, PRE, TAIL + PRE))
@@ -101,35 +105,43 @@
         for copy in halo_copies:
             copy.start()
 
+    def dense(value):
+        low = lax.broadcasted_iota(jnp.int32, (8, value.shape[1]), 0) < 4
+        up, down = pltpu.roll(value[16:24], 4, 0), pltpu.roll(value[24:32], 4, 0)
+        return [value[:8], jnp.where(low, value[8:16], up), jnp.where(low, up, down)]
+
+    cot16[...] = jnp.zeros_like(cot16)
+    cot16[:12] = cot_in[...]
+    for p, both_y in enumerate(((0, 3), (1, 2))):
+        for k in (0, 1):
+            for j, yy in enumerate(both_y):
+                tiles = []
+                for m in range(NZ // 2):
+                    pair = [
+                        cot16[:, pl.ds(((2 * m + n) * NY + yy) * 256 + k * 128, 128)].astype(F32) for n in (0, 1)
+                    ]
+                    tiles += dense(jnp.concatenate(pair, axis=0))
+                cot_ref[p, k, :, j * 128 : (j + 1) * 128] = jnp.concatenate(tiles, axis=0).astype(BF16)
+    c_here = cp.at[tp, cot_rows(t)]
+    c_sib = remote(cot_ref.at[ps, 1 - c], c_here, sib_s.at[1], sib_r.at[1], sib)
+    c_pair = [
+        remote(cot_ref.at[1 - ps, c], c_here, cy_s.at[0], cy_r.at[0], part_same),
+        remote(cot_ref.at[1 - ps, 1 - c], c_here, cy_s.at[1], cy_r.at[1], part_other),
+    ]
+    c_own = pltpu.make_async_copy(cot_ref.at[ps, c], c_here, own_sem.at[1])
+    for copy in [c_sib, c_own] + c_pair:
+        copy.start()
     def z_right(zs, h):
-        return remote(unit(zs, y, h), unit(zs, y, h), z_s.at[0, zs, h], z_r.at[zs, h], dright)
+        return remote(unit(zs, js, h), unit(zs, js, h), z_s.at[0, zs, h], z_r.at[zs, h], dright)
 
     def z_left(zs, h):
-        return remote(unit(zs, y, h), unit(zs, y, h), z_s.at[1, zs, h], z_r.at[zs, h], dleft)
-
-    def y_plus(zs, yy, h, kind):
-        return remote(unit(zs, yy, h), unit(zs, yy, h), y_s.at[kind, zs, h], y_r.at[kind, zs, h], yp)
-
-    def y_minus(zs, yy, h, kind):
-        return remote(unit(zs, yy, h), unit(zs, yy, h), y_s.at[kind, zs, h], y_r.at[kind, zs, h], ym)
+        return remote(unit(zs, js, h), unit(zs, js, h), z_s.at[1, zs, h], z_r.at[zs, h], dleft)
+
+    def across(zs, j, h):
+        return remote(unit(zs, j, h), unit(zs, j, h), y_s.at[zs, h], y_r.at[zs, h], wy)
 
     def spread(zs, h):
-        y_plus(zs, y, h, 0).start()
-        y_minus(zs, y, h, 1).start()
-
-    def relay(zs, h):
-        y_plus(zs, (y + 3) % NY, h, 0).wait_recv()
-        y_minus(zs, (y + 1) % NY, h, 1).wait_recv()
-
-        upward = (h == 0) & (zs != zl)
-
-        @pl.when(upward)
-        def _():
-            y_plus(zs, (y + 3) % NY, h, 2).start()
-
-        @pl.when(jnp.logical_not(upward))
-        def _():
-            y_minus(zs, (y + 1) % NY, h, 2).start()
+        across(zs, js, h).start()
 
     def cot_z(k):
         piece = zh * (2 * NX) + x * 2 + k
@@ -159,8 +171,10 @@
         spread(zl, h)
         if h is c:
             c_own.wait()
+            c_pair[0].wait_recv()
         else:
             c_sib.wait()
+            c_pair[1].wait_recv()
         cot_z(h).start()
         for n in range(3):
             cot_x(zh, h, n).start()
@@ -188,11 +202,6 @@
         for i in range(count):
             at = 12 * i
             yield (value[at : at + 16] if at % 8 == 0 else shifted[at - 4 : at + 12]).astype(BF16)
-
-    def dense(value):
-        low = lax.broadcasted_iota(jnp.int32, (8, value.shape[1]), 0) < 4
-        up, down = pltpu.roll(value[16:24], 4, 0), pltpu.roll(value[24:32], 4, 0)
-        return [value[:8], jnp.where(low, value[8:16], up), jnp.where(low, up, down)]
 
     def convolve(source, first, step, lanes):
         def residue(r, value):
@@ -229,16 +238,17 @@
             gated[16 * i : 16 * i + 16, lanes] = rows16
 
     def weight(zs, k):
-        return jnp.concatenate([wg[zs * NY + yy, k * rows : (k + 1) * rows] for yy in range(NY)], axis=1)
+        return jnp.concatenate([wg[zs * 2 + j, k * rows : (k + 1) * rows] for j in (0, 1)], axis=1)
 
     def forward(zs):
         value = jnp.dot(both[0], weight(zs, 0), preferred_element_type=F32)
         value = value + jnp.dot(both[1], weight(zs, 1), preferred_element_type=F32)
         for xx in range(NX):
             groups = []
-            for half in (0, 1):
-                at = (half * NX + xx) * 32
-                groups += dense(value[at : at + 32])
+            for which in (0, 1):
+                for half in (0, 1):
+                    at = which * 256 + (half * NX + xx) * 32
+                    groups += dense(value[at : at + 32])
             out[zs, xx] = jnp.concatenate(groups, axis=0).astype(BF16)
         for n in range(3):
             out_x(zs, n).start()
@@ -255,8 +265,8 @@
             out_x(zs, n).wait_recv()
             value = value + arrived[zs, n].astype(F32)
         for half in (0, 1):
-            own = value[24 * half : 24 * half + 24]
-            sums[half, zs] = jnp.concatenate([own[:, :256], own[:, 256:]], axis=0).astype(BF16)
+            at = 24 * half
+            sums[half, zs] = jnp.concatenate([value[at : at + 24], value[48 + at : 72 + at]], axis=0).astype(BF16)
 
     def out_far(zs):
         return remote(sums.at[1 - zh, zs], far.at[zs], f_s.at[zs], f_r.at[zs], zpart)
@@ -273,20 +283,23 @@
         def _(n):
             act(nth(n))
 
-    x_sib = remote(gated, both.at[c], sib_s.at[2], sib_r.at[2], sib)
-    x_own = pltpu.make_async_copy(gated, both.at[c], own_sem.at[2])
+    x_here = both.at[c, token_rows(t)]
+    x_out = [
+        remote(gated, x_here, xp_s.at[n], xp_r.at[n], to) for n, to in enumerate((sib, part_same, part_other))
+    ]
+    x_own = pltpu.make_async_copy(gated, x_here, own_sem.at[2])
 
     def forward_done(step):
-        return jnp.maximum(0, jnp.minimum(2 * (step - 2), step - 1))
+        return jnp.maximum(0, jnp.minimum(2 * (step - 2), step))
 
     def backward_done(step):
-        return jnp.maximum(0, jnp.minimum(3 * (step - 5), step - 1))
-
-    @pl.loop(1, NZ + 2)
+        return jnp.maximum(0, jnp.minimum(3 * (step - 5), step))
+
+    @pl.loop(1, NZ + 1)
     def _(step):
-        for h in order:
-            @pl.when((zl - step >= 0) & (step < NZ))
-            def _(h=h):
+        def pass_on(h):
+            @pl.when(zl - step >= 0)
+            def _():
                 z_right(zl - step, h).wait_recv()
 
                 @pl.when(zl < NZ - 1)
@@ -294,33 +307,20 @@
                     z_right(zl - step, h).start()
 
             @pl.when(zl + step < NZ)
-            def _(h=h):
+            def _():
                 z_left(zl + step, h).wait_recv()
 
                 @pl.when(zl > 0)
                 def _():
                     z_left(zl + step, h).start()
 
-        def pass_on(zs):
-            for h in order:
-                relay(zs, h)
-
-        def relayed(zs):
-            for h in (0, 1):
-                y_plus(zs, (y + 2) % NY, h, 2).wait_recv()
-
-        @pl.when(step < NZ)
-        def _():
-            for h in order:
+            @pl.when(step < NZ)
+            def _():
                 spread(nth(step), h)
 
-        @pl.when(step <= NZ)
-        def _():
-            pass_on(nth(step - 1))
-
-        @pl.when(step >= 2)
-        def _():
-            relayed(nth(step - 2))
+        pass_on(c)
+        for h in order:
+            across(nth(step - 1), 1 - js, h).wait_recv()
 
         @pl.when((step == 1) & (ctx > 0))
         def _():
@@ -335,8 +335,18 @@
 
         @pl.when(step == 2)
         def _():
-            x_sib.start()
             x_own.start()
+            for copy in x_out:
+                copy.start()
+
+        @pl.when(step == 3)
+        def _():
+            x_own.wait()
+            for copy in x_out:
+                copy.wait()
+
+        each(forward_done(step - 1), forward_done(step), forward)
+        pass_on(1 - c)
 
         @pl.when(step == 4)
         def _():
@@ -345,11 +355,6 @@
                 for n in range(3):
                     cot_x(1 - zh, k, n).start()
 
-        @pl.when(step == 3)
-        def _():
-            x_own.wait()
-            x_sib.wait()
-
         @pl.when(step == 6)
         def _():
             for k in (0, 1):
@@ -359,32 +364,44 @@
 
             @pl.loop(0, 4 * NX)
             def _(piece):
-                at = pl.ds(pl.multiple_of(piece * 16, 16), 16)
-                for zs, rows16 in enumerate(spaced(cp[piece].astype(F32), NZ)):
-                    cg[zs, at] = rows16
-
-        each(forward_done(step - 1), forward_done(step), forward)
+                for which in (0, 1):
+                    at = pl.ds(pl.multiple_of(which * 256 + piece * 16, 16), 16)
+                    value = cp[piece, 96 * which : 96 * which + 96].astype(F32)
+                    for zs, rows16 in enumerate(spaced(value, NZ)):
+                        cg[zs, at] = rows16
+
         each(backward_done(step - 1), backward_done(step), backward)
-        each(forward_done(step - 3), forward_done(step - 2), collect)
+        each(forward_done(step - 2), forward_done(step - 1), collect)
 
         @pl.when(step >= NZ - 1)
         def _():
-            each(jnp.where(step == NZ - 1, 0, forward_done(step - 3)), forward_done(step - 2), lambda zs: out_far(zs).start())
-
-    gsend[...] = acc[1 - c].astype(BF16)
-    g_sib = remote(gsend, grecv, sib_s.at[3], sib_r.at[3], sib)
-    g_sib.start()
-
-    g_sib.wait()
+            each(jnp.where(step == NZ - 1, 0, forward_done(step - 2)), forward_done(step - 1), lambda zs: out_far(zs).start())
+
+    def packed(k, which, lanes):
+        tiles = []
+        for m in range(8):
+            at = pl.ds(pl.multiple_of(which * 256 + 32 * m, 32), 32)
+            tiles += dense(acc[k, at, lanes])
+        return jnp.concatenate(tiles, axis=0)
+
+    g_out = [
+        remote(gsend.at[n], grecv.at[n], g_s.at[n], g_r.at[n], to)
+        for n, to in enumerate((part_same, part_other, sib))
+    ]
+    for n, (k, which) in enumerate(((c, 1 - t), (1 - c, 1 - t), (1 - c, t))):
+        for l in range(4):
+            lanes = slice(l * 128, (l + 1) * 128)
+            gsend[n, :, lanes] = packed(k, which, lanes).astype(BF16)
+        g_out[n].start()
+
+    for copy in g_out:
+        copy.wait()
 
     def gradients(l):
         lanes = lane(l)
-        tiles = []
-        for m in range(8):
-            at = 32 * m
-            block = acc[c, at : at + 32, lanes] + grecv[at : at + 32, lanes].astype(F32)
-            tiles += dense(block)
-        mixed_grad = jnp.concatenate(tiles, axis=0)
+        mixed_grad = packed(c, t, lanes)
+        for n in range(3):
+            mixed_grad = mixed_grad + grecv[n, :, lanes].astype(F32)
         long_grad = mixed_grad * qf[:, lanes]
         query_grad = mixed_grad * ls[:, lanes]
         glb[:T, lanes] = long_grad
@@ -526,11 +543,18 @@
     for zs in range(NZ):
         out_far(zs).wait()
         value = sums[zh, zs].astype(F32) + far[zs].astype(F32)
-        value = jnp.concatenate([value[:24], value[24:]], axis=1)
-        for k, rows16 in enumerate(spaced(value, 2)):
-            near[k, zs] = rows16
-    m_sib = remote(near.at[1 - c], come.at[c], sib_s.at[4], sib_r.at[4], sib)
-    m_sib.start()
+        for which in (0, 1):
+            for k, rows16 in enumerate(spaced(value[24 * which : 24 * which + 24], 2)):
+                near[which, k, zs] = rows16
+    m_out = [
+        remote(near.at[which, k], come.at[ps, c], m_s.at[n], m_r.at[n], to)
+        for n, (which, k, to) in enumerate(
+            ((t, 1 - c, sib), (1 - t, c, part_same), (1 - t, 1 - c, part_other))
+        )
+    ]
+    for copy in m_out:
+        copy.start()
+    come[ps, c] = near[t, c]
 
     value = tmine[...].astype(F32)
     for n in range(NZ - 1):
@@ -541,20 +565,14 @@
         back_z(n).wait()
     for n in range(3):
         back_y(n).start()
-    m_sib.wait()
-    for k in (0, 1):
-        for zs in range(NZ):
-            for yy in range(NY):
-                at = (zs * NY + yy) * 256
-                lanes = slice(yy * 128, (yy + 1) * 128)
-
-                @pl.when(c == k)
-                def _(zs=zs, lanes=lanes, at=at, k=k):
-                    mixed_ref[:, at + k * 128 : at + (k + 1) * 128] = near[k, zs, :, lanes][:12]
-
-                @pl.when(c != k)
-                def _(zs=zs, lanes=lanes, at=at, k=k):
-                    mixed_ref[:, at + k * 128 : at + (k + 1) * 128] = come[k, zs, :, lanes][:12]
+    for copy in m_out:
+        copy.wait()
+    for p, both_y in enumerate(((0, 3), (1, 2))):
+        for k in (0, 1):
+            for zs in range(NZ):
+                for j, yy in enumerate(both_y):
+                    at = (zs * NY + yy) * 256 + k * 128
+                    mixed_ref[:, at : at + 128] = come[p, k, zs, :, j * 128 : (j + 1) * 128][:12]
 
     for n in range(3):
         back_y(n).wait()
@@ -586,9 +604,7 @@
     @pl.loop(0, NZ)
     def _(zs):
         for h in (0, 1):
-            y_plus(zs, y, h, 0).wait_send()
-            y_minus(zs, y, h, 1).wait_send()
-            y_plus(zs, y, h, 2).wait_send()
+            across(zs, js, h).wait_send()
 
             @pl.when((zs <= zl) & (zl < NZ - 1))
             def _():
@@ -601,6 +617,8 @@
         for n in range(3):
             out_x(zs, n).wait_send()
 
+    for copy in c_pair:
+        copy.wait_send()
     for k in (0, 1):
         cot_z(k).wait_send()
         for half in (0, 1):
@@ -631,19 +649,19 @@
         in_specs=[vmem] * 5,
         out_specs=(vmem,) * 4,
         scratch_shapes=[
-            f32(*taps.shape), f32(8, 16, wide),
-            b16(NZ * NY, 2 * rows, 128), b16(4 * NX, 96, 512), b16(NZ, 256, 512), b16(TAIL + 2 * PRE, wide),
+            b16(16, cot.shape[1]), b16(2, 2, 96, 256), f32(*taps.shape), f32(8, 16, wide),
+            b16(NZ * 2, 2 * rows, 128), b16(4 * NX, 192, 256), b16(NZ, 512, 256), b16(TAIL + 2 * PRE, wide),
             f32(T, wide), f32(T, wide), f32(T, wide), f32(T, wide), f32(8, T + PRE, wide),
-            b16(256, wide), b16(2, 256, wide), f32(2, 256, wide),
-            b16(NZ, NX, 48, 512), b16(NZ, 3, 48, 512), b16(256, wide), b16(256, wide),
-            b16(2, NZ, 48, 256), b16(NZ, 48, 256), b16(2, NZ, 16, 512), b16(2, NZ, 16, 512),
+            b16(256, wide), b16(2, 512, wide), f32(2, 512, wide),
+            b16(NZ, NX, 96, 256), b16(NZ, 3, 96, 256), b16(3, T, wide), b16(3, T, wide),
+            b16(2, NZ, 48, 256), b16(NZ, 48, 256), b16(2, 2, NZ, 16, 256), b16(2, 2, NZ, 16, 256),
             b16(NY, NZ + 1, 16, 128),
             f32(T + 128, wide), f32(8, T + 128, 128), f32(T, wide), f32(T, wide), f32(T, wide),
             b16(128 + TAIL, wide), b16(128 + TAIL, wide), b16(2, TAIL, wide), b16(2, TAIL, wide), f32(16, wide),
             b16(NY, NZ, 16, 128), b16(NZ, 16, 128), b16(3, NZ, 16, 128), b16(NZ - 1, 16, 128), f32(8, 16, wide),
             b16(NY, 16, 128), b16(16, 128), b16(3, 16, 128), b16(NZ - 1, 16, 128),
-            dma((3,)), dma((5,)), dma((5,)),
-            dma((2, NZ, 2)), dma((NZ, 2)), dma((3, NZ, 2)), dma((3, NZ, 2)),
+            dma((3,)), dma((2,)), dma((2,)), dma((2,)), dma((2,)), dma((3,)), dma((3,)), dma((3,)), dma((3,)), dma((3,)), dma((3,)),
+            dma((2, NZ, 2)), dma((NZ, 2)), dma((NZ, 2)), dma((NZ, 2)),
             dma((2, 2, 3)), dma((2, 2, 3)), dma((NZ, 3)), dma((NZ, 3)), dma((2,)), dma((2,)), dma((NZ,)), dma((NZ,)), dma((5,)), dma((5,)),
             dma((3,)), dma((3,)), dma((NZ - 1,)), dma((NZ - 1,)), dma((NZ - 1,)), dma((NZ - 1,)),
             dma((NZ - 1,)), dma((NZ - 1,)), dma((3,)), dma((3,)), dma((3,)), dma((3,)),
@@ -656,11 +674,7 @@
 
 
 def body(branch_inputs, feat_taps, long_filter, out_weight, cotangent):
-    own_rows = cotangent.shape[0]
-    cot_halves = (
-        cotangent.reshape(own_rows, NZ, NY, 2, 128).transpose(3, 1, 0, 2, 4).reshape(2, NZ * own_rows, 512)
-    )
-    return block(branch_inputs, feat_taps, long_filter, out_weight, cot_halves)
+    return block(branch_inputs, feat_taps, long_filter, out_weight, cotangent)
 
 
 def solution(mesh):

time: 154 us -> 144 us (0.935)
  Pallas kernels: 147 us -> 138 us
  local copies, waits for them, and re-layouts: 6.88 us -> 4.98 us
    pallas_call x1, Pallas kernels: 147 us -> 138 us  [block(): pl.pallas_call(block_kernel, out_shape=(jax.ShapeDtypeStruct((12, 8192),...]
    reshape x3 -> x0, local copies, waits for them, and re-layouts: 1.9 us -> none  [body(): cotangent.reshape(own_rows, NZ, NY, 2, 128).transpose(3, 1, 0, 2, 4)]
where the time goes in v6:
time: 144 us
  Pallas kernels  138 us (96%)
  local copies, waits for them, and re-layouts  4.98 us (3%)
    pallas_call x1, Pallas kernels, block(): pl.pallas_call(block_kernel, out_shape=(jax.ShapeDtypeStruct((12, 8192),...  138 us
    unnamed x8, local copies, waits for them, and re-layouts  4.98 us

profile of v6, /device:TPU:6, one launch (start us, length us, event | category | flops | bytes accessed | tf_op | source)
XLA Modules:
  0.0 143.9 jit_solution(1079849921824994367)
XLA Ops:
  0.6 138.3 %hyena_block.1 = (bf16[12,8192]{1,0:T(8,128)(2,1)}, bf16[3,192,512]{2,1,0:T(8,128)(2,1)}, f32[128,512]{1,0:T(8,128)}, f32[3,3,512]{2,1,0:T(4,128)}) custom-call(bf16[3,192,512]{2,1,0:T(8,128)(2,1)} %br_ref.1, bf16[3,3,512]{2,1,0:T(4,128)(2,1)} %ftaps_ref.1, f32[128,512]{1,0:T(8,128)} %filt_ref.1, bf16[512,256]{1,0:T(8,128)(2,1)} %w_ref.1, ...), custom_call_target="tpu_custom_call" | custom-call | tf_op jit(solution)/shard_map/hyena_block/pallas_call | solution.py:641
  139.0 1.7 %copy.13 = bf16[12,8192]{1,0:T(8,128)(2,1)} copy(bf16[12,8192]{1,0:T(8,128)(2,1)} %get-tuple-element.8) | data formatting | bytes 393216
  140.6 0.0 copy-start
  140.6 2.0 %copy.14 = bf16[3,192,512]{2,1,0:T(8,128)(2,1)} copy(bf16[3,192,512]{2,1,0:T(8,128)(2,1)} %get-tuple-element.9) | data formatting | bytes 1179648
  142.6 0.0 copy-done
  142.6 0.0 copy-start.1
  142.6 0.7 copy.15
  143.3 0.0 copy-done.1
  143.3 0.6 copy.16
Async XLA Ops:
  140.6 2.0 %copy-start = (f32[128,512]{1,0:T(8,128)S(1)}, f32[128,512]{1,0:T(8,128)}, u32[]{:S(2)}) copy-start(f32[128,512]{1,0:T(8,128)} %get-tuple-element.10) | copy-start | bytes 786436
  142.6 0.7 copy-start.1

commit v7 on v6

--- a/solution.py
+++ b/solution.py
@@ -290,7 +290,7 @@
     x_own = pltpu.make_async_copy(gated, x_here, own_sem.at[2])
 
     def forward_done(step):
-        return jnp.maximum(0, jnp.minimum(2 * (step - 2), step))
+        return jnp.maximum(0, jnp.minimum(2 * (step - 4), step))
 
     def backward_done(step):
         return jnp.maximum(0, jnp.minimum(3 * (step - 5), step))
@@ -327,19 +327,17 @@
             for copy in halo_copies:
                 copy.wait_recv()
 
-        @pl.when(step <= 2)
+        @pl.when(step <= 4)
         def _():
-            @pl.loop(2 * step - 2, 2 * step)
-            def _(l):
-                features(l)
-
-        @pl.when(step == 2)
+            features(step - 1)
+
+        @pl.when(step == 4)
         def _():
             x_own.start()
             for copy in x_out:
                 copy.start()
 
-        @pl.when(step == 3)
+        @pl.when(step == 5)
         def _():
             x_own.wait()
             for copy in x_out:

time: 144 us -> 141 us (0.979)
  Pallas kernels: 138 us -> 135 us
    pallas_call x1, Pallas kernels: 138 us -> 135 us  [block(): pl.pallas_call(block_kernel, out_shape=(jax.ShapeDtypeStruct((12, 8192),...]
where the time goes in v7:
time: 141 us
  Pallas kernels  135 us (96%)
  local copies, waits for them, and re-layouts  4.98 us (4%)
    pallas_call x1, Pallas kernels, block(): pl.pallas_call(block_kernel, out_shape=(jax.ShapeDtypeStruct((12, 8192),...  135 us
    unnamed x8, local copies, waits for them, and re-layouts  4.98 us

profile of v7, /device:TPU:6, one launch (start us, length us, event | category | flops | bytes accessed | tf_op | source)
XLA Modules:
  0.0 140.8 jit_solution(11234115798553688508)
XLA Ops:
  0.6 135.2 %hyena_block.1 = (bf16[12,8192]{1,0:T(8,128)(2,1)}, bf16[3,192,512]{2,1,0:T(8,128)(2,1)}, f32[128,512]{1,0:T(8,128)}, f32[3,3,512]{2,1,0:T(4,128)}) custom-call(bf16[3,192,512]{2,1,0:T(8,128)(2,1)} %br_ref.1, bf16[3,3,512]{2,1,0:T(4,128)(2,1)} %ftaps_ref.1, f32[128,512]{1,0:T(8,128)} %filt_ref.1, bf16[512,256]{1,0:T(8,128)(2,1)} %w_ref.1, ...), custom_call_target="tpu_custom_call" | custom-call | tf_op jit(solution)/shard_map/hyena_block/pallas_call | solution.py:639
  135.9 1.7 %copy.13 = bf16[12,8192]{1,0:T(8,128)(2,1)} copy(bf16[12,8192]{1,0:T(8,128)(2,1)} %get-tuple-element.8) | data formatting | bytes 393216
  137.5 0.0 copy-start
  137.5 2.0 %copy.14 = bf16[3,192,512]{2,1,0:T(8,128)(2,1)} copy(bf16[3,192,512]{2,1,0:T(8,128)(2,1)} %get-tuple-element.9) | data formatting | bytes 1179648
  139.5 0.0 copy-done
  139.5 0.0 copy-start.1
  139.5 0.7 copy.15
  140.2 0.0 copy-done.1
  140.2 0.6 copy.16
Async XLA Ops:
  137.5 2.0 %copy-start = (f32[128,512]{1,0:T(8,128)S(1)}, f32[128,512]{1,0:T(8,128)}, u32[]{:S(2)}) copy-start(f32[128,512]{1,0:T(8,128)} %get-tuple-element.10) | copy-start | bytes 786436
  139.5 0.7 copy-start.1
